TPU v7x, 32 devices: a whole 2x2x4 slice. The times are simulated.
32 devices in a mesh: section: 2 (over core), dp: 16 (over z, y, x).
Axes of the slice: x: 2, y: 2, z: 4, core: 2. Of those that a mesh axis runs over, the one named last changes fastest.
Arguments:
- raw_series: bfloat16 [128, 1024, 144], P('dp'), may hold values from -12 to 12
- series_ids: int32 [128], P('dp'), may hold values from 0 to 127, each once
- series_median: float32 [128], replicated, may hold values from -4 to 4
- series_scale: float32 [128], replicated, may hold values from 0.5 to 4
- cotangent: bfloat16 [128, 1024, 144], P('dp'), may hold values from -6 to 6
- norm_gains: float32 [2, 2, 144], P('section'), may hold values from 0.1 to 1.9
- qkv_weight: bfloat16 [2, 144, 432], P('section'), may hold values from -0.5 to 0.5
- out_weight: bfloat16 [2, 144, 144], P('section'), may hold values from -1.5 to 1.5
- gate_up_weight: bfloat16 [2, 144, 768], P('section'), may hold values from -0.5 to 0.5
- down_weight: bfloat16 [2, 384, 144], P('section'), may hold values from -0.3125 to 0.3125
Outputs:
- layer_outputs: bfloat16 [2, 128, 1024, 144], P('section', 'dp')
- input_grads: float32 [2, 128, 1024, 144], P('section', 'dp')
- grad_norm_gains: float32 [2, 2, 144], P('section')
- grad_qkv_weight: float32 [2, 144, 432], P('section')
- grad_out_weight: float32 [2, 144, 144], P('section')
- grad_gate_up_weight: float32 [2, 144, 768], P('section')
- grad_down_weight: float32 [2, 384, 144], P('section')
Inputs may be any that keep to these rules, and one draw needn't show every extreme that they name: `series_ids`: each series number appears exactly once.
All inputs are finite; a program needn't handle non-finite values.
Results may differ from a plain program's by a relative error of at most 0.012.
Values may be sent and summed in bfloat16 or wider, within the bound.
A program may use at most 256 MiB of HBM per device.

v0:
```python
import jax
import jax.numpy as jnp
from jax import lax
from jax.sharding import PartitionSpec as P

HEAD = 16


epsilon = 1e-06
highest = lax.Precision.HIGHEST
bfloat = jnp.bfloat16
single = jnp.float32


def from_behind(block, axis, distance):
    devices = range(lax.axis_size(axis))
    route = [(i - distance, i) for i in devices if i - distance in devices]
    return lax.ppermute(block, axis, route)


def rotary_tables(length, head_width):
    half_width = head_width // 2
    frequency = 10000.0 ** (-jnp.arange(half_width, dtype=single) / half_width)
    angles = jnp.arange(length, dtype=single)[:, None] * frequency[None, :]
    return (jnp.cos(angles)[:, None, :], jnp.sin(angles)[:, None, :])


def rotate(values, cosine_table, sine_table):
    half_width = values.shape[-1] // 2
    leading = values[..., :half_width]
    trailing = values[..., half_width:]
    return jnp.concatenate(
        [
            leading * cosine_table - trailing * sine_table,
            trailing * cosine_table + leading * sine_table,
        ],
        axis=-1,
    )


def rms_scale(values):
    return lax.rsqrt(jnp.mean(values * values, axis=-1, keepdims=True) + epsilon)


def rms_backward(grad_normed, values, inverse, gain):
    scaled = grad_normed * gain
    grad_gain = jnp.sum(grad_normed * values * inverse, axis=0)
    grad_values = inverse * scaled - values * inverse**3 * jnp.mean(
        scaled * values, axis=-1, keepdims=True
    )
    return (grad_values, grad_gain)


def causal_mask(length, first_row, end_row):
    positions = jnp.arange(length)
    return (positions[None, :end_row] <= positions[first_row:end_row, None])[None]


def layer_forward(inputs, weights, tables):
    norm_gains, qkv_weight, out_weight, gate_up_weight, down_weight = weights
    cosine_table, sine_table = tables
    length, model_width = inputs.shape
    head_count = model_width // HEAD
    first_inverse = rms_scale(inputs)
    normed = (inputs * first_inverse * norm_gains[0]).astype(bfloat)
    projected = jnp.dot(normed, qkv_weight, preferred_element_type=single).reshape(
        length, 3, head_count, HEAD
    )
    queries = rotate(projected[:, 0], cosine_table, sine_table).astype(bfloat)
    key_rows = rotate(projected[:, 1], cosine_table, sine_table).astype(bfloat)
    values = projected[:, 2].astype(bfloat)
    block_rows = min(512, length)
    outputs = []
    totals = []
    for first_row in range(0, length, block_rows):
        end_row = first_row + block_rows
        scores = jnp.einsum(
            "qhe,khe->hqk",
            queries[first_row:end_row],
            key_rows[:end_row],
            preferred_element_type=single,
        ) * HEAD ** (-0.5)
        scores = jnp.where(causal_mask(length, first_row, end_row), scores, -1e30)
        largest = jnp.max(scores, axis=-1, keepdims=True)
        exponent = jnp.exp(scores - largest)
        row_total = jnp.sum(exponent, axis=-1, keepdims=True)
        probabilities = (exponent / row_total).astype(bfloat)
        outputs.append(
            jnp.einsum(
                "hqk,khe->qhe", probabilities, values[:end_row], preferred_element_type=single
            )
        )
        totals.append(largest + jnp.log(row_total))
    attended = jnp.concatenate(outputs, axis=0).reshape(length, model_width).astype(bfloat)
    log_totals = jnp.concatenate(totals, axis=1)
    residual = inputs + jnp.dot(attended, out_weight, preferred_element_type=single)
    second_inverse = rms_scale(residual)
    normed_mid = (residual * second_inverse * norm_gains[1]).astype(bfloat)
    gate_up = jnp.dot(normed_mid, gate_up_weight, preferred_element_type=single)
    hidden_width = down_weight.shape[0]
    gate_pre = gate_up[:, :hidden_width]
    up_pre = gate_up[:, hidden_width:]
    activated = (gate_pre * jax.nn.sigmoid(gate_pre) * up_pre).astype(bfloat)
    result = residual + jnp.dot(activated, down_weight, preferred_element_type=single)
    stored = (
        inputs,
        first_inverse,
        normed,
        queries,
        key_rows,
        values,
        log_totals,
        attended,
        residual,
        second_inverse,
        normed_mid,
        gate_pre,
        up_pre,
        activated,
    )
    return (result, stored)


def layer_backward(grad_result, stored, weights, tables):
    norm_gains, qkv_weight, out_weight, gate_up_weight, down_weight = weights
    cosine_table, sine_table = tables
    (
        inputs,
        first_inverse,
        normed,
        queries,
        key_rows,
        values,
        log_totals,
        attended,
        residual,
        second_inverse,
        normed_mid,
        gate_pre,
        up_pre,
        activated,
    ) = stored
    length, model_width = inputs.shape
    head_count = model_width // HEAD
    branch_grad = grad_result.astype(bfloat)
    grad_down = jnp.dot(activated.T, branch_grad, preferred_element_type=single)
    grad_activated = jnp.dot(branch_grad, down_weight.T, preferred_element_type=single)
    sigmoid_gate = jax.nn.sigmoid(gate_pre)
    grad_gate = grad_activated * up_pre * sigmoid_gate * (1.0 + gate_pre * (1.0 - sigmoid_gate))
    grad_upper = grad_activated * gate_pre * sigmoid_gate
    grad_gate_up = jnp.concatenate([grad_gate, grad_upper], axis=1).astype(bfloat)
    grad_gu_weight = jnp.dot(normed_mid.T, grad_gate_up, preferred_element_type=single)
    grad_mid = jnp.dot(grad_gate_up, gate_up_weight.T, preferred_element_type=single)
    grad_residual, grad_second = rms_backward(grad_mid, residual, second_inverse, norm_gains[1])
    grad_residual = grad_residual + grad_result
    attention_grad = grad_residual.astype(bfloat)
    grad_out = jnp.dot(attended.T, attention_grad, preferred_element_type=single)
    grad_attended = (
        jnp.dot(attention_grad, out_weight.T, preferred_element_type=single)
        .astype(bfloat)
        .reshape(length, head_count, HEAD)
    )
    block_rows = min(512, length)
    factor = HEAD ** (-0.5)
    query_parts = []
    grad_keys = jnp.zeros((length, head_count, HEAD), single)
    grad_values = jnp.zeros((length, head_count, HEAD), single)
    for first_row in range(0, length, block_rows):
        end_row = first_row + block_rows
        scores = (
            jnp.einsum(
                "qhe,khe->hqk",
                queries[first_row:end_row],
                key_rows[:end_row],
                preferred_element_type=single,
            )
            * factor
        )
        scores = jnp.where(causal_mask(length, first_row, end_row), scores, -1e30)
        probabilities = jnp.exp(scores - log_totals[:, first_row:end_row])
        grad_probs = jnp.einsum(
            "qhe,khe->hqk",
            grad_attended[first_row:end_row],
            values[:end_row],
            preferred_element_type=single,
        )
        centre = jnp.sum(probabilities * grad_probs, axis=-1, keepdims=True)
        grad_scores = (probabilities * (grad_probs - centre)).astype(bfloat)
        query_parts.append(
            jnp.einsum(
                "hqk,khe->qhe", grad_scores, key_rows[:end_row], preferred_element_type=single
            )
            * factor
        )
        grad_keys = grad_keys.at[:end_row].add(
            jnp.einsum(
                "hqk,qhe->khe",
                grad_scores,
                queries[first_row:end_row],
                preferred_element_type=single,
            )
            * factor
        )
        grad_values = grad_values.at[:end_row].add(
            jnp.einsum(
                "hqk,qhe->khe",
                probabilities.astype(bfloat),
                grad_attended[first_row:end_row],
                preferred_element_type=single,
            )
        )
    grad_queries = jnp.concatenate(query_parts, axis=0)
    grad_query_pre = rotate(grad_queries, cosine_table, -sine_table)
    grad_key_pre = rotate(grad_keys, cosine_table, -sine_table)
    grad_projected = (
        jnp.stack([grad_query_pre, grad_key_pre, grad_values], axis=1)
        .reshape(length, 3 * model_width)
        .astype(bfloat)
    )
    grad_qkv = jnp.dot(normed.T, grad_projected, preferred_element_type=single)
    grad_normed = jnp.dot(grad_projected, qkv_weight.T, preferred_element_type=single)
    grad_inputs, grad_first = rms_backward(grad_normed, inputs, first_inverse, norm_gains[0])
    grad_inputs = grad_inputs + grad_residual
    return (
        grad_inputs,
        (jnp.stack([grad_first, grad_second]), grad_qkv, grad_out, grad_gu_weight, grad_down),
    )


def on_device(
    raw_series,
    series_ids,
    series_median,
    series_scale,
    cotangent,
    norm_gains,
    qkv_weight,
    out_weight,
    gate_up_weight,
    down_weight,
):
    micro_count = raw_series.shape[0]
    length = raw_series.shape[1]
    weights = (norm_gains[0], qkv_weight[0], out_weight[0], gate_up_weight[0], down_weight[0])
    tables = rotary_tables(length, HEAD)
    is_first = lax.axis_index("section") == 0
    matches = (series_ids[:, None] == jnp.arange(series_median.shape[0])[None, :]).astype(single)
    centers = jnp.dot(matches, series_median, precision=highest)
    spreads = jnp.dot(matches, series_scale, precision=highest)
    normalized = (raw_series.astype(single) - centers[:, None, None]) / spreads[:, None, None]

    def forward_tick(arriving, moment):
        own_rows = lax.dynamic_index_in_dim(
            normalized, jnp.minimum(moment, micro_count - 1), 0, keepdims=False
        )
        inputs = jnp.where(is_first, own_rows, arriving.astype(single))
        result, stored = layer_forward(inputs, weights, tables)
        sending = result.astype(bfloat)
        passed = from_behind(sending, "section", 1)
        return (passed, (sending, stored))

    start_zero = jnp.zeros((length, raw_series.shape[2]), bfloat)
    last_arrival, (sent_all, retained_all) = lax.scan(
        forward_tick, start_zero, jnp.arange(micro_count + 1)
    )
    outputs_here = jnp.where(is_first, sent_all[:micro_count], sent_all[1:])
    zero_grads = tuple((jnp.zeros(member.shape, single) for member in weights))

    def backward_tick(state_pair, moment):
        arriving, running = state_pair
        which = jnp.clip(jnp.where(is_first, moment - 1, moment + 1), 0, micro_count)
        usable = jnp.where(is_first, moment >= 1, moment < micro_count).astype(single)
        incoming = lax.dynamic_index_in_dim(
            cotangent, jnp.minimum(moment, micro_count - 1), 0, keepdims=False
        ).astype(single)
        grad_result = jnp.where(is_first, arriving.astype(single), incoming)
        restored = jax.tree.map(
            lambda member: lax.dynamic_index_in_dim(member, which, 0, keepdims=False), retained_all
        )
        grad_inputs, gradients = layer_backward(grad_result, restored, weights, tables)
        gain_grad, qkv_grad, out_grad, gu_grad, down_grad = tuple(
            (member * usable for member in gradients)
        )
        gain_grad, qkv_grad, out_grad, gu_grad, down_grad = lax.psum(
            (gain_grad, qkv_grad, out_grad, gu_grad, down_grad), "dp"
        )
        running = tuple(
            (
                total_term + member
                for total_term, member in zip(
                    running, (gain_grad, qkv_grad, out_grad, gu_grad, down_grad)
                )
            )
        )
        passed = from_behind(grad_inputs.astype(bfloat), "section", -1)
        return ((passed, running), grad_inputs)

    (last_grad, totals), grad_all = lax.scan(
        backward_tick, (start_zero, zero_grads), jnp.arange(micro_count + 1)
    )
    gain_total, qkv_total, out_total, gu_total, down_total = totals
    grad_here = jnp.where(is_first, grad_all[1:] / spreads[:, None, None], grad_all[:micro_count])
    return (
        outputs_here[None],
        grad_here[None],
        gain_total[None],
        qkv_total[None],
        out_total[None],
        gu_total[None],
        down_total[None],
    )


def solution(mesh):
    placed = (
        P("dp", None, None),
        P("dp"),
        P(),
        P(),
        P("dp", None, None),
        P("section", None, None),
        P("section", None, None),
        P("section", None, None),
        P("section", None, None),
        P("section", None, None),
    )
    return jax.shard_map(
        on_device,
        mesh=mesh,
        in_specs=placed,
        out_specs=(
            P("section", "dp", None, None),
            P("section", "dp", None, None),
            P("section", None, None),
            P("section", None, None),
            P("section", None, None),
            P("section", None, None),
            P("section", None, None),
        ),
        check_vma=False,
    )
```

profile of v0, /device:TPU:0, one launch (start us, length us, event | category | flops | bytes accessed | tf_op | source)
XLA Modules:
  0.0 2549.1 jit_solution(10824538955196905736)
XLA Ops:
  21.7 456.8 %while.78 = (s32[]{:T(128)}, bf16[1024,144]{0,1:T(8,128)(2,1)S(1)}, bf16[9,1024,144]{1,2,0:T(8,128)(2,1)S(1)}, f32[9,1024,144]{1,2,0:T(8,128)}, f32[9,1024,1]{1,...) while((s32[]{:T(128)}, bf16[1024,144]{0,1:T(8,128)(2,1)S(1)}, ...), condition=%wide.region_7.8_spmd.clone.clone.clone, body=%wide.region_0.7_spmd.clone.clone.clone.sunk | while | flops 1058646016 | bytes 166045312 | solution.py:263
  483.2 2051.3 %while.79 = (s32[]{:T(128)}, bf16[1024,144]{0,1:T(8,128)(2,1)S(1)}, f32[2,144]{1,0:T(2,128)S(1)}, f32[144,432]{1,0:T(8,128)}, f32[144,144]{1,0:T(8,128)}, /*inde...) while((s32[]{:T(128)}, bf16[1024,144]{0,1:T(8,128)(2,1)S(1)}, ...), condition=%wide.region_20.21_spmd.clone.clone.clone.clone, body=%wide.region_8.20_spmd.clone.clone.clone.clone.sunk | while | flops 2281070592 | bytes 350450240 | solution.py:298
  557.5 13.6 multiply_reduce_fusion.10
  614.0 43.1 %psum.76 = f32[2,144]{1,0:T(2,128)S(1)} all-reduce(f32[2,144]{1,0:T(2,128)S(1)} %maximum_multiply_fusion.2), channel_id=1, replica_groups=mesh['section'=2,'dp'=16] {'dp'}, use_global_device_ids=true, to_apply=%region_15.15 | all-reduce | flops 288 | bytes 2304 | tf_op jit(solution)/shard_map/while/body/eval_jaxpr/psum | solution.py:284
  657.1 67.4 %all-reduce.7.cloned.1.call-done = (f32[144,432]{1,0:T(8,128)}, f32[144,144]{1,0:T(8,128)}, f32[144,768]{1,0:T(8,128)}, f32[384,144]{0,1:T(8,128)}) async-done(((f32[144,432]{1,0:T(8,128)}, f32[144,144]{1,0:T(8,128)}, f32[144,768]{1,0:T(8,128)}, f32[384,144]{0,1:T(8,128)}), (f32[144,432]{1,0:T(8,128)}, f32[144,144]{1,0:T(8,128)}, f32[144,768]{1,0:T(8,128)}, ...) | async-done | bytes 995344 | tf_op jit(solution)/shard_map/while/body/eval_jaxpr/psum | solution.py:284
  786.0 13.6 multiply_reduce_fusion.10
  842.4 40.1 %psum.76 = f32[2,144]{1,0:T(2,128)S(1)} all-reduce(f32[2,144]{1,0:T(2,128)S(1)} %maximum_multiply_fusion.2), channel_id=1, replica_groups=mesh['section'=2,'dp'=16] {'dp'}, use_global_device_ids=true, to_apply=%region_15.15 | all-reduce | flops 288 | bytes 2304 | tf_op jit(solution)/shard_map/while/body/eval_jaxpr/psum | solution.py:284
  882.6 67.4 %all-reduce.7.cloned.1.call-done = (f32[144,432]{1,0:T(8,128)}, f32[144,144]{1,0:T(8,128)}, f32[144,768]{1,0:T(8,128)}, f32[384,144]{0,1:T(8,128)}) async-done(((f32[144,432]{1,0:T(8,128)}, f32[144,144]{1,0:T(8,128)}, f32[144,768]{1,0:T(8,128)}, f32[384,144]{0,1:T(8,128)}), (f32[144,432]{1,0:T(8,128)}, f32[144,144]{1,0:T(8,128)}, f32[144,768]{1,0:T(8,128)}, ...) | async-done | bytes 995344 | tf_op jit(solution)/shard_map/while/body/eval_jaxpr/psum | solution.py:284
  1068.0 40.1 %psum.76 = f32[2,144]{1,0:T(2,128)S(1)} all-reduce(f32[2,144]{1,0:T(2,128)S(1)} %maximum_multiply_fusion.2), channel_id=1, replica_groups=mesh['section'=2,'dp'=16] {'dp'}, use_global_device_ids=true, to_apply=%region_15.15 | all-reduce | flops 288 | bytes 2304 | tf_op jit(solution)/shard_map/while/body/eval_jaxpr/psum | solution.py:284
  1108.2 67.4 %all-reduce.7.cloned.1.call-done = (f32[144,432]{1,0:T(8,128)}, f32[144,144]{1,0:T(8,128)}, f32[144,768]{1,0:T(8,128)}, f32[384,144]{0,1:T(8,128)}) async-done(((f32[144,432]{1,0:T(8,128)}, f32[144,144]{1,0:T(8,128)}, f32[144,768]{1,0:T(8,128)}, f32[384,144]{0,1:T(8,128)}), (f32[144,432]{1,0:T(8,128)}, f32[144,144]{1,0:T(8,128)}, f32[144,768]{1,0:T(8,128)}, ...) | async-done | bytes 995344 | tf_op jit(solution)/shard_map/while/body/eval_jaxpr/psum | solution.py:284
  1293.7 40.1 %psum.76 = f32[2,144]{1,0:T(2,128)S(1)} all-reduce(f32[2,144]{1,0:T(2,128)S(1)} %maximum_multiply_fusion.2), channel_id=1, replica_groups=mesh['section'=2,'dp'=16] {'dp'}, use_global_device_ids=true, to_apply=%region_15.15 | all-reduce | flops 288 | bytes 2304 | tf_op jit(solution)/shard_map/while/body/eval_jaxpr/psum | solution.py:284
  1333.8 67.4 %all-reduce.7.cloned.1.call-done = (f32[144,432]{1,0:T(8,128)}, f32[144,144]{1,0:T(8,128)}, f32[144,768]{1,0:T(8,128)}, f32[384,144]{0,1:T(8,128)}) async-done(((f32[144,432]{1,0:T(8,128)}, f32[144,144]{1,0:T(8,128)}, f32[144,768]{1,0:T(8,128)}, f32[384,144]{0,1:T(8,128)}), (f32[144,432]{1,0:T(8,128)}, f32[144,144]{1,0:T(8,128)}, f32[144,768]{1,0:T(8,128)}, ...) | async-done | bytes 995344 | tf_op jit(solution)/shard_map/while/body/eval_jaxpr/psum | solution.py:284
  1462.9 13.6 multiply_reduce_fusion.10
  1519.3 40.1 %psum.76 = f32[2,144]{1,0:T(2,128)S(1)} all-reduce(f32[2,144]{1,0:T(2,128)S(1)} %maximum_multiply_fusion.2), channel_id=1, replica_groups=mesh['section'=2,'dp'=16] {'dp'}, use_global_device_ids=true, to_apply=%region_15.15 | all-reduce | flops 288 | bytes 2304 | tf_op jit(solution)/shard_map/while/body/eval_jaxpr/psum | solution.py:284
  1559.4 67.4 %all-reduce.7.cloned.1.call-done = (f32[144,432]{1,0:T(8,128)}, f32[144,144]{1,0:T(8,128)}, f32[144,768]{1,0:T(8,128)}, f32[384,144]{0,1:T(8,128)}) async-done(((f32[144,432]{1,0:T(8,128)}, f32[144,144]{1,0:T(8,128)}, f32[144,768]{1,0:T(8,128)}, f32[384,144]{0,1:T(8,128)}), (f32[144,432]{1,0:T(8,128)}, f32[144,144]{1,0:T(8,128)}, f32[144,768]{1,0:T(8,128)}, ...) | async-done | bytes 995344 | tf_op jit(solution)/shard_map/while/body/eval_jaxpr/psum | solution.py:284
  1688.5 13.6 multiply_reduce_fusion.10
  1744.9 40.2 %psum.76 = f32[2,144]{1,0:T(2,128)S(1)} all-reduce(f32[2,144]{1,0:T(2,128)S(1)} %maximum_multiply_fusion.2), channel_id=1, replica_groups=mesh['section'=2,'dp'=16] {'dp'}, use_global_device_ids=true, to_apply=%region_15.15 | all-reduce | flops 288 | bytes 2304 | tf_op jit(solution)/shard_map/while/body/eval_jaxpr/psum | solution.py:284
  1785.0 67.4 %all-reduce.7.cloned.1.call-done = (f32[144,432]{1,0:T(8,128)}, f32[144,144]{1,0:T(8,128)}, f32[144,768]{1,0:T(8,128)}, f32[384,144]{0,1:T(8,128)}) async-done(((f32[144,432]{1,0:T(8,128)}, f32[144,144]{1,0:T(8,128)}, f32[144,768]{1,0:T(8,128)}, f32[384,144]{0,1:T(8,128)}), (f32[144,432]{1,0:T(8,128)}, f32[144,144]{1,0:T(8,128)}, f32[144,768]{1,0:T(8,128)}, ...) | async-done | bytes 995344 | tf_op jit(solution)/shard_map/while/body/eval_jaxpr/psum | solution.py:284
  1970.5 40.2 %psum.76 = f32[2,144]{1,0:T(2,128)S(1)} all-reduce(f32[2,144]{1,0:T(2,128)S(1)} %maximum_multiply_fusion.2), channel_id=1, replica_groups=mesh['section'=2,'dp'=16] {'dp'}, use_global_device_ids=true, to_apply=%region_15.15 | all-reduce | flops 288 | bytes 2304 | tf_op jit(solution)/shard_map/while/body/eval_jaxpr/psum | solution.py:284
  2010.7 67.4 %all-reduce.7.cloned.1.call-done = (f32[144,432]{1,0:T(8,128)}, f32[144,144]{1,0:T(8,128)}, f32[144,768]{1,0:T(8,128)}, f32[384,144]{0,1:T(8,128)}) async-done(((f32[144,432]{1,0:T(8,128)}, f32[144,144]{1,0:T(8,128)}, f32[144,768]{1,0:T(8,128)}, f32[384,144]{0,1:T(8,128)}), (f32[144,432]{1,0:T(8,128)}, f32[144,144]{1,0:T(8,128)}, f32[144,768]{1,0:T(8,128)}, ...) | async-done | bytes 995344 | tf_op jit(solution)/shard_map/while/body/eval_jaxpr/psum | solution.py:284
  2196.1 40.1 %psum.76 = f32[2,144]{1,0:T(2,128)S(1)} all-reduce(f32[2,144]{1,0:T(2,128)S(1)} %maximum_multiply_fusion.2), channel_id=1, replica_groups=mesh['section'=2,'dp'=16] {'dp'}, use_global_device_ids=true, to_apply=%region_15.15 | all-reduce | flops 288 | bytes 2304 | tf_op jit(solution)/shard_map/while/body/eval_jaxpr/psum | solution.py:284
  2236.2 67.4 %all-reduce.7.cloned.1.call-done = (f32[144,432]{1,0:T(8,128)}, f32[144,144]{1,0:T(8,128)}, f32[144,768]{1,0:T(8,128)}, f32[384,144]{0,1:T(8,128)}) async-done(((f32[144,432]{1,0:T(8,128)}, f32[144,144]{1,0:T(8,128)}, f32[144,768]{1,0:T(8,128)}, f32[384,144]{0,1:T(8,128)}), (f32[144,432]{1,0:T(8,128)}, f32[144,144]{1,0:T(8,128)}, f32[144,768]{1,0:T(8,128)}, ...) | async-done | bytes 995344 | tf_op jit(solution)/shard_map/while/body/eval_jaxpr/psum | solution.py:284
  2421.7 40.1 %psum.76 = f32[2,144]{1,0:T(2,128)S(1)} all-reduce(f32[2,144]{1,0:T(2,128)S(1)} %maximum_multiply_fusion.2), channel_id=1, replica_groups=mesh['section'=2,'dp'=16] {'dp'}, use_global_device_ids=true, to_apply=%region_15.15 | all-reduce | flops 288 | bytes 2304 | tf_op jit(solution)/shard_map/while/body/eval_jaxpr/psum | solution.py:284
  2461.8 67.4 %all-reduce.7.cloned.1.call-done = (f32[144,432]{1,0:T(8,128)}, f32[144,144]{1,0:T(8,128)}, f32[144,768]{1,0:T(8,128)}, f32[384,144]{0,1:T(8,128)}) async-done(((f32[144,432]{1,0:T(8,128)}, f32[144,144]{1,0:T(8,128)}, f32[144,768]{1,0:T(8,128)}, f32[384,144]{0,1:T(8,128)}), (f32[144,432]{1,0:T(8,128)}, f32[144,144]{1,0:T(8,128)}, f32[144,768]{1,0:T(8,128)}, ...) | async-done | bytes 995344 | tf_op jit(solution)/shard_map/while/body/eval_jaxpr/psum | solution.py:284
  (1261 shorter events, 1452.7 us)
Async XLA Ops:
  62.2 10.2 collective-permute-start
  113.8 9.2 collective-permute-start
  164.5 9.3 collective-permute-start
  215.2 9.2 collective-permute-start
  417.7 9.2 collective-permute-start
  468.3 9.2 collective-permute-start
  501.1 223.3 %all-reduce.7.cloned.1.call-start = ((), (), s32[]{:S(2)}) async-start(), calls=%async_computation | async-start | bytes 2211840 | tf_op jit(solution)/shard_map/while/body/eval_jaxpr/psum | solution.py:284
  612.6 44.4 %collective-permute-start.1 = (bf16[1024,144]{0,1:T(8,128)(2,1)S(1)}, bf16[1024,144]{0,1:T(8,128)(2,1)S(1)}, u32[]{:S(2)}, u32[]{:S(2)}) collective-permute-start(bf16[1024,144]{0,1:T(8,128)(2,1)S(1)} %get-tuple-element.1950), channel_id=1, source_target_pairs={{16,0},{17,1},{18,2},{19,3},{20,4},{21,5},{22,6},{23,7},{24,8},{25... | collective-permute-start | bytes 884744 | tf_op jit(solution)/shard_map/while/body/eval_jaxpr/ppermute | solution.py:18
  729.6 220.4 %all-reduce.7.cloned.1.call-start = ((), (), s32[]{:S(2)}) async-start(), calls=%async_computation | async-start | bytes 2211840 | tf_op jit(solution)/shard_map/while/body/eval_jaxpr/psum | solution.py:284
  841.1 41.4 %collective-permute-start.1 = (bf16[1024,144]{0,1:T(8,128)(2,1)S(1)}, bf16[1024,144]{0,1:T(8,128)(2,1)S(1)}, u32[]{:S(2)}, u32[]{:S(2)}) collective-permute-start(bf16[1024,144]{0,1:T(8,128)(2,1)S(1)} %get-tuple-element.1950), channel_id=1, source_target_pairs={{16,0},{17,1},{18,2},{19,3},{20,4},{21,5},{22,6},{23,7},{24,8},{25... | collective-permute-start | bytes 884744 | tf_op jit(solution)/shard_map/while/body/eval_jaxpr/ppermute | solution.py:18
  955.3 220.4 %all-reduce.7.cloned.1.call-start = ((), (), s32[]{:S(2)}) async-start(), calls=%async_computation | async-start | bytes 2211840 | tf_op jit(solution)/shard_map/while/body/eval_jaxpr/psum | solution.py:284
  1066.7 41.5 %collective-permute-start.1 = (bf16[1024,144]{0,1:T(8,128)(2,1)S(1)}, bf16[1024,144]{0,1:T(8,128)(2,1)S(1)}, u32[]{:S(2)}, u32[]{:S(2)}) collective-permute-start(bf16[1024,144]{0,1:T(8,128)(2,1)S(1)} %get-tuple-element.1950), channel_id=1, source_target_pairs={{16,0},{17,1},{18,2},{19,3},{20,4},{21,5},{22,6},{23,7},{24,8},{25... | collective-permute-start | bytes 884744 | tf_op jit(solution)/shard_map/while/body/eval_jaxpr/ppermute | solution.py:18
  1180.9 220.4 %all-reduce.7.cloned.1.call-start = ((), (), s32[]{:S(2)}) async-start(), calls=%async_computation | async-start | bytes 2211840 | tf_op jit(solution)/shard_map/while/body/eval_jaxpr/psum | solution.py:284
  1292.4 41.4 %collective-permute-start.1 = (bf16[1024,144]{0,1:T(8,128)(2,1)S(1)}, bf16[1024,144]{0,1:T(8,128)(2,1)S(1)}, u32[]{:S(2)}, u32[]{:S(2)}) collective-permute-start(bf16[1024,144]{0,1:T(8,128)(2,1)S(1)} %get-tuple-element.1950), channel_id=1, source_target_pairs={{16,0},{17,1},{18,2},{19,3},{20,4},{21,5},{22,6},{23,7},{24,8},{25... | collective-permute-start | bytes 884744 | tf_op jit(solution)/shard_map/while/body/eval_jaxpr/ppermute | solution.py:18
  1406.5 220.4 %all-reduce.7.cloned.1.call-start = ((), (), s32[]{:S(2)}) async-start(), calls=%async_computation | async-start | bytes 2211840 | tf_op jit(solution)/shard_map/while/body/eval_jaxpr/psum | solution.py:284
  1518.0 41.5 %collective-permute-start.1 = (bf16[1024,144]{0,1:T(8,128)(2,1)S(1)}, bf16[1024,144]{0,1:T(8,128)(2,1)S(1)}, u32[]{:S(2)}, u32[]{:S(2)}) collective-permute-start(bf16[1024,144]{0,1:T(8,128)(2,1)S(1)} %get-tuple-element.1950), channel_id=1, source_target_pairs={{16,0},{17,1},{18,2},{19,3},{20,4},{21,5},{22,6},{23,7},{24,8},{25... | collective-permute-start | bytes 884744 | tf_op jit(solution)/shard_map/while/body/eval_jaxpr/ppermute | solution.py:18
  1632.1 220.4 %all-reduce.7.cloned.1.call-start = ((), (), s32[]{:S(2)}) async-start(), calls=%async_computation | async-start | bytes 2211840 | tf_op jit(solution)/shard_map/while/body/eval_jaxpr/psum | solution.py:284
  1743.6 41.5 %collective-permute-start.1 = (bf16[1024,144]{0,1:T(8,128)(2,1)S(1)}, bf16[1024,144]{0,1:T(8,128)(2,1)S(1)}, u32[]{:S(2)}, u32[]{:S(2)}) collective-permute-start(bf16[1024,144]{0,1:T(8,128)(2,1)S(1)} %get-tuple-element.1950), channel_id=1, source_target_pairs={{16,0},{17,1},{18,2},{19,3},{20,4},{21,5},{22,6},{23,7},{24,8},{25... | collective-permute-start | bytes 884744 | tf_op jit(solution)/shard_map/while/body/eval_jaxpr/ppermute | solution.py:18
  1857.7 220.4 %all-reduce.7.cloned.1.call-start = ((), (), s32[]{:S(2)}) async-start(), calls=%async_computation | async-start | bytes 2211840 | tf_op jit(solution)/shard_map/while/body/eval_jaxpr/psum | solution.py:284
  1969.1 41.5 %collective-permute-start.1 = (bf16[1024,144]{0,1:T(8,128)(2,1)S(1)}, bf16[1024,144]{0,1:T(8,128)(2,1)S(1)}, u32[]{:S(2)}, u32[]{:S(2)}) collective-permute-start(bf16[1024,144]{0,1:T(8,128)(2,1)S(1)} %get-tuple-element.1950), channel_id=1, source_target_pairs={{16,0},{17,1},{18,2},{19,3},{20,4},{21,5},{22,6},{23,7},{24,8},{25... | collective-permute-start | bytes 884744 | tf_op jit(solution)/shard_map/while/body/eval_jaxpr/ppermute | solution.py:18
  2083.3 220.4 %all-reduce.7.cloned.1.call-start = ((), (), s32[]{:S(2)}) async-start(), calls=%async_computation | async-start | bytes 2211840 | tf_op jit(solution)/shard_map/while/body/eval_jaxpr/psum | solution.py:284
  2194.8 41.5 %collective-permute-start.1 = (bf16[1024,144]{0,1:T(8,128)(2,1)S(1)}, bf16[1024,144]{0,1:T(8,128)(2,1)S(1)}, u32[]{:S(2)}, u32[]{:S(2)}) collective-permute-start(bf16[1024,144]{0,1:T(8,128)(2,1)S(1)} %get-tuple-element.1950), channel_id=1, source_target_pairs={{16,0},{17,1},{18,2},{19,3},{20,4},{21,5},{22,6},{23,7},{24,8},{25... | collective-permute-start | bytes 884744 | tf_op jit(solution)/shard_map/while/body/eval_jaxpr/ppermute | solution.py:18
  2308.9 220.4 %all-reduce.7.cloned.1.call-start = ((), (), s32[]{:S(2)}) async-start(), calls=%async_computation | async-start | bytes 2211840 | tf_op jit(solution)/shard_map/while/body/eval_jaxpr/psum | solution.py:284
  2420.4 41.5 %collective-permute-start.1 = (bf16[1024,144]{0,1:T(8,128)(2,1)S(1)}, bf16[1024,144]{0,1:T(8,128)(2,1)S(1)}, u32[]{:S(2)}, u32[]{:S(2)}) collective-permute-start(bf16[1024,144]{0,1:T(8,128)(2,1)S(1)} %get-tuple-element.1950), channel_id=1, source_target_pairs={{16,0},{17,1},{18,2},{19,3},{20,4},{21,5},{22,6},{23,7},{24,8},{25... | collective-permute-start | bytes 884744 | tf_op jit(solution)/shard_map/while/body/eval_jaxpr/ppermute | solution.py:18
  (192 other events, 6881.8 us)
Sparse Core Ops, SparseCore 0:
  608.3 116.0 all-reduce.6
  836.8 113.1 all-reduce.6
  1062.4 113.1 all-reduce.6
  1288.0 113.1 all-reduce.6
  1513.6 113.1 all-reduce.6
  1739.2 113.1 all-reduce.6
  1964.8 113.2 all-reduce.6
  2190.4 113.1 all-reduce.6
  2416.0 113.1 all-reduce.6
where the time goes:
time: 2570 us; the launch traced here: 2550 us
  matrix products  819 us (32%)
  waiting for transfers between devices  607 us (24%)
  other arithmetic  505 us (20%)
  blocking collectives  364 us (14%)
  local copies, waits for them, and re-layouts  152 us (6%)
  loops' own time  56.8 us (2%)
  starting transfers between devices  30.5 us (1%)
    psum x9, waiting for transfers between devices, backward_tick(): lax.psum((gain_grad, qkv_grad, out_grad, gu_grad, down_grad), 'dp')  607 us
    psum x9, blocking collectives, backward_tick(): lax.psum((gain_grad, qkv_grad, out_grad, gu_grad, down_grad), 'dp')  364 us
    convert_element_type x18, other arithmetic, layer_backward(): grad_scores = (probabilities * (grad_probs - centre)).astype(bfloat)  223 us
    dot_general x18, matrix products, layer_backward(): jnp.einsum('qhe,khe->hqk', grad_attended[first_row:end_row], values[:end_...  178 us
    dot_general x18, matrix products, layer_backward(): jnp.einsum('qhe,khe->hqk', queries[first_row:end_row], key_rows[:end_row]...  113 us
    dot_general x18, matrix products, layer_backward(): jnp.einsum('hqk,qhe->khe', probabilities.astype(bfloat), grad_attended[fi...  99.6 us
    reduce_sum x18, other arithmetic, layer_forward(): row_total = jnp.sum(exponent, axis=-1, keepdims=True)  95.1 us
    dynamic_update_slice x63, other arithmetic, on_device(): lax.scan(forward_tick, start_zero, jnp.arange(micro_count + 1))  90.4 us
  transfers between devices with their start and end apart: 27, of which 9 were waited for; matrix products, arithmetic and copies ran while one was open for 4% of the time, Pallas kernels for 0%

commit v1 on v0

v1 whole, which is shorter than its diff:
```python
import functools
import math

import jax
import jax.numpy as jnp
import numpy as np
from jax import lax
from jax.experimental import pallas as pl
from jax.experimental.pallas import tpu as pltpu
from jax.sharding import PartitionSpec as P

HEAD = 16
HALF = HEAD // 2
TILE = 256
EPSILON = 1e-06
LOG2E = math.log2(math.e)
QKV_REST = 48
OUT_REST = 16
MESH = pl.DeviceIdType.MESH
bfloat = jnp.bfloat16
single = jnp.float32


def dot(left, right):
    return jnp.dot(left, right, preferred_element_type=single)


def dot_nt(left, right):
    return lax.dot_general(left, right, (((1,), (1,)), ((), ())), preferred_element_type=single)


def rms_scale(values):
    return lax.rsqrt(jnp.mean(values * values, axis=0, keepdims=True) + EPSILON)


def rms_backward(grad_normed, values, inverse, gain):
    scaled = grad_normed * gain
    centre = jnp.mean(scaled * values, axis=0, keepdims=True)
    grad_values = inverse * scaled - values * (inverse * inverse * inverse * centre)
    product = grad_normed * values * inverse
    partial = product[:, :128]
    for start in range(128, product.shape[1], 128):
        partial = partial + product[:, start : start + 128]
    return grad_values, partial


def causal(block):
    rows = lax.broadcasted_iota(jnp.int32, block.shape, 0)
    columns = lax.broadcasted_iota(jnp.int32, block.shape, 1)
    return rows <= columns


def tile_start(j):
    return j * (j + 1) // 2 * TILE


def train_kernel(
    heads,
    hidden,
    place,
    series_ids,
    median,
    scale,
    raw,
    cotangent,
    own_gains,
    own_qkv,
    own_out,
    own_gate_up,
    own_down_t,
    other_gains,
    other_qkv,
    other_out,
    other_gate_up,
    other_down_t,
    cosine,
    sine,
    kept_out,
    kept_grad,
    sent_out,
    sent_grad,
    own_total,
    other_total,
    gains,
    qkv_t,
    out_t,
    gate_up_t,
    down_t,
    qkv_w,
    out_w,
    gate_up_w,
    down_w,
    grad_gains,
    grad_qkv,
    grad_out,
    grad_gate_up,
    grad_down,
    inputs,
    inverse1,
    normed,
    queries,
    keys,
    values,
    rows_major,
    exponents,
    attended32,
    reciprocal,
    attended,
    residual,
    inverse2,
    mid,
    gate_up,
    activated,
    grad,
    grad_low,
    grad_pre,
    grad_res_low,
    grad_att,
    grad_q,
    grad_k,
    grad_v,
    grad_proj,
):
    step = pl.program_id(0)
    section = place[0]
    series = place[1] + step
    number = series_ids[series]
    centre = median[number]
    inverse_spread = 1.0 / scale[number]
    width, length = inputs.shape[1:]
    tiles = length // TILE
    query_factor = HEAD**-0.5 * LOG2E

    @pl.when(step == 0)
    def _():
        for ref in (grad_gains, grad_qkv, grad_out, grad_gate_up, grad_down):
            ref[...] = jnp.zeros_like(ref)
        row = lax.broadcasted_iota(jnp.int32, (2, heads, HEAD, length), 2)
        values[:, :, HEAD:, :] = jnp.where(row < 2, 1.0, 0.0).astype(bfloat)
        flipped = lambda w: w.astype(single).T.astype(bfloat)
        for l, (gain, qkv, out, both, down) in (
            (section, (own_gains, own_qkv, own_out, own_gate_up, own_down_t)),
            (1 - section, (other_gains, other_qkv, other_out, other_gate_up, other_down_t)),
        ):
            for part in range(2):
                row = jnp.broadcast_to(gain[part : part + 1, :], (128, width))
                gains[l, part] = row.T
            qkv_w[l] = qkv[...]
            qkv_t[l] = flipped(qkv[...])
            out_w[l] = out[...]
            out_t[l] = flipped(out[...])
            gate_up_w[l] = both[...]
            gate_up_t[l] = flipped(both[...])
            down_t[l] = down[...]
            down_w[l] = flipped(down[...])

    def gain_of(l, part):
        return jnp.concatenate([gains[l, part]] * (TILE // 128), axis=1)

    inputs[0] = (raw[0].astype(single) - centre) * inverse_spread
    grad[...] = cotangent[0].astype(single)

    def rotated(block, cs, sign):
        a, b = block[:, :HALF], block[:, HALF:]
        cos, sin = cosine[:, cs], sine[:, cs] * sign
        return jnp.concatenate([a * cos - b * sin, b * cos + a * sin], axis=1)

    def forward(l, carry):
        largest = jnp.zeros((1, 1, TILE), single)
        largest_q = jnp.zeros((heads, 1, TILE), single)
        largest_k = jnp.zeros((heads, 1, TILE), single)
        for c in range(tiles):
            cs = slice(c * TILE, (c + 1) * TILE)
            u = inputs[l, :, cs]
            inv = rms_scale(u)
            inverse1[l, :, cs] = inv
            low = (u * inv * gain_of(l, 0)).astype(bfloat)
            normed[l, :, cs] = low
            projected = dot(qkv_t[l], low).reshape(3 * heads, HEAD, TILE)
            q = (rotated(projected[:heads], cs, 1.0) * query_factor).astype(bfloat)
            k = rotated(projected[heads : 2 * heads], cs, 1.0)
            queries[l, :, :, cs] = q
            keys[l, :, :, cs] = k.astype(bfloat)
            values[l, :, :HEAD, cs] = projected[2 * heads :].astype(bfloat)
            for h in range(heads):
                rows_major[h, cs, :HEAD] = k[h].T.astype(bfloat)
            q32 = q.astype(single)
            k32 = k.astype(bfloat).astype(single)
            largest_q = jnp.maximum(largest_q, jnp.sum(q32 * q32, axis=1, keepdims=True))
            largest_k = jnp.maximum(largest_k, jnp.sum(k32 * k32, axis=1, keepdims=True))
        bound = jnp.max(jnp.max(largest_q, axis=2) * jnp.max(largest_k, axis=2))

        def finish(h, j, total):
            js = slice(j * TILE, (j + 1) * TILE)
            inverse = 1.0 / total[HEAD : HEAD + 1]
            out = total[:HEAD] * inverse
            reciprocal[l, h, :, js] = inverse
            attended32[l, h, :, js] = out
            attended[l, h, :, js] = out.astype(bfloat)

        small = bound <= 1e4

        @pl.when(small)
        def _():
            group = 3
            ahead = 3

            def some(hh, carry):
                work = [
                    (hh * group + g, j, k)
                    for g in range(group)
                    for j in range(tiles)
                    for k in range(j + 1)
                ]
                scores = {}

                def score(n):
                    h, j, k = work[n]
                    scores[n] = dot(
                        rows_major[h, k * TILE : (k + 1) * TILE, :HEAD],
                        queries[l, h, :, j * TILE : (j + 1) * TILE],
                    )

                for n in range(ahead):
                    score(n)
                total = None
                for n, (h, j, k) in enumerate(work):
                    if n + ahead < len(work):
                        score(n + ahead)
                    e = jnp.exp2(scores.pop(n))
                    if k == j:
                        e = jnp.where(causal(e), e, 0.0)
                    e = e.astype(bfloat)
                    first = tile_start(j) + k * TILE
                    exponents[l, h, first : first + TILE, :] = e
                    part = dot(values[l, h, :, k * TILE : (k + 1) * TILE], e)
                    total = part if k == 0 else total + part
                    if k == j:
                        finish(h, j, total)
                return carry

            lax.fori_loop(0, heads // group, some, 0)

        @pl.when(jnp.logical_not(small))
        def _():
            def one(h, carry):
                for j in range(tiles):
                    count = (j + 1) * TILE
                    js = slice(j * TILE, (j + 1) * TILE)
                    score = dot(rows_major[h, :count, :HEAD], queries[l, h, :, js])
                    rows = lax.broadcasted_iota(jnp.int32, score.shape, 0)
                    columns = lax.broadcasted_iota(jnp.int32, score.shape, 1) + j * TILE
                    score = jnp.where(rows <= columns, score, -1e30)
                    e = jnp.exp2(score - jnp.max(score, axis=0, keepdims=True)).astype(bfloat)
                    exponents[l, h, tile_start(j) : tile_start(j) + count, :] = e
                    finish(h, j, dot(values[l, h, :, :count], e))
                return carry

            lax.fori_loop(0, heads, one, 0)

        for c in range(tiles):
            cs = slice(c * TILE, (c + 1) * TILE)
            res = inputs[l, :, cs] + dot(out_t[l], attended[l, :, :, cs].reshape(width, TILE))
            residual[l, :, cs] = res
            inv = rms_scale(res)
            inverse2[l, :, cs] = inv
            low = (res * inv * gain_of(l, 1)).astype(bfloat)
            mid[l, :, cs] = low
            both = dot(gate_up_t[l], low)
            gate_up[l, :, cs] = both
            gate, up = both[:hidden], both[hidden:]
            act = (gate * jax.nn.sigmoid(gate) * up).astype(bfloat)
            activated[l, :, cs] = act
            result = res + dot(down_t[l], act)
            low = result.astype(bfloat)

            @pl.when(l == section)
            def _():
                kept_out[0, :, cs] = low

            @pl.when(l != section)
            def _():
                sent_out[0, :, cs] = low

            @pl.when(l == 0)
            def _():
                inputs[1, :, cs] = low.astype(single)

        return carry

    lax.fori_loop(0, 2, forward, 0)

    def backward(turn, carry):
        l = 1 - turn
        slot = lax.rem(l + section, 2)
        for c in range(tiles):
            cs = slice(c * TILE, (c + 1) * TILE)
            g = grad[:, cs]
            low = g.astype(bfloat)
            grad_low[:, cs] = low
            grad_act = dot(down_w[l], low)
            gate, up = gate_up[l, :hidden, cs], gate_up[l, hidden:, cs]
            sig = jax.nn.sigmoid(gate)
            inner = grad_act * sig
            grad_gate = inner * up * (1.0 + gate * (1.0 - sig))
            grad_up = inner * gate
            pre = jnp.concatenate([grad_gate, grad_up], axis=0).astype(bfloat)
            grad_pre[:, cs] = pre
            grad_mid = dot(gate_up_w[l], pre)
            res, inv = residual[l, :, cs], inverse2[l, :, cs]
            grad_res, partial = rms_backward(grad_mid, res, inv, gain_of(l, 1))
            grad_gains[slot, 1] += partial
            grad_res = grad_res + g
            grad[:, cs] = grad_res
            low = grad_res.astype(bfloat)
            grad_res_low[:, cs] = low
            back = dot(out_w[l], low).astype(bfloat).astype(single).reshape(heads, HEAD, TILE)
            inverse = reciprocal[l, :, :, cs]
            mean = jnp.sum(back * attended32[l, :, :, cs], axis=1, keepdims=True) * -inverse
            coarse = mean.astype(bfloat).astype(single)
            row = lax.broadcasted_iota(jnp.int32, (heads, HEAD, TILE), 1)
            extra = jnp.where(row == 0, coarse, jnp.where(row == 1, mean - coarse, 0.0))
            grad_att[:, :, cs] = jnp.concatenate([back * inverse, extra], axis=1).astype(bfloat)
        grad_down[slot] += dot_nt(grad_low[...], activated[l])
        grad_gate_up[slot] += dot_nt(mid[l], grad_pre[...])
        grad_out[slot] += dot_nt(attended[l].reshape(width, length), grad_res_low[...])

        for h in range(heads):
            rows_major[h] = values[l, h].astype(single).T.astype(bfloat)

        group = 3
        ahead = 3

        def some(hh, carry):
            work = [
                (g, j, k) for g in range(group) for j in range(tiles) for k in range(j + 1)
            ]
            products = {}

            def product(n):
                g, j, k = work[n]
                products[n] = dot(
                    rows_major[hh * group + g, k * TILE : (k + 1) * TILE, :],
                    grad_att[hh * group + g, :, j * TILE : (j + 1) * TILE],
                )

            for n in range(ahead):
                product(n)
            sums = {}

            def add(key, value):
                sums[key] = sums[key] + value if key in sums else value

            for n, (g, j, k) in enumerate(work):
                h = hh * group + g
                if n + ahead < len(work):
                    product(n + ahead)
                first = tile_start(j) + k * TILE
                e = exponents[l, h, first : first + TILE, :]
                grad_score = e * products.pop(n).astype(bfloat)
                js, ks = slice(j * TILE, (j + 1) * TILE), slice(k * TILE, (k + 1) * TILE)
                add(("q", j), dot(keys[l, h, :, ks], grad_score))
                add(("k", k), dot_nt(queries[l, h, :, js], grad_score))
                add(("v", k), dot_nt(grad_att[h, :HEAD, js], e))
                if (j, k) == (tiles - 1, tiles - 1):
                    for t in range(tiles):
                        ts = slice(t * TILE, (t + 1) * TILE)
                        grad_q[h, :, ts] = sums.pop(("q", t))
                        grad_k[h, :, ts] = sums.pop(("k", t))
                        grad_v[h, :, ts] = sums.pop(("v", t))
            return carry

        lax.fori_loop(0, heads // group, some, 0)

        for c in range(tiles):
            cs = slice(c * TILE, (c + 1) * TILE)
            dq = rotated(grad_q[:, :, cs] * HEAD**-0.5, cs, -1.0)
            dk = rotated(grad_k[:, :, cs] * (1.0 / LOG2E), cs, -1.0)
            low = jnp.concatenate([dq, dk, grad_v[:, :, cs]], axis=0).astype(bfloat)
            low = low.reshape(3 * width, TILE)
            grad_proj[:, cs] = low
            grad_normed = dot(qkv_w[l], low)
            u, inv = inputs[l, :, cs], inverse1[l, :, cs]
            grad_u, partial = rms_backward(grad_normed, u, inv, gain_of(l, 0))
            grad_gains[slot, 0] += partial
            grad_u = grad_u + grad[:, cs]
            grad[:, cs] = grad_u.astype(bfloat).astype(single)
            grad_u = grad_u * jnp.where(l == 0, inverse_spread, 1.0)

            @pl.when(l == section)
            def _():
                kept_grad[0, :, cs] = grad_u

            @pl.when(l != section)
            def _():
                sent_grad[0, :, cs] = grad_u.astype(bfloat)

        grad_qkv[slot] += dot_nt(normed[l], grad_proj[...])
        return carry

    lax.fori_loop(0, 2, backward, 0)

    @pl.when(step == pl.num_programs(0) - 1)
    def _():
        for slot, total in ((0, own_total), (1, other_total)):
            blocks = []
            for ref in (grad_gate_up, grad_down, grad_qkv, grad_out):
                blocks += [ref[slot, :, n : n + 128] for n in range(0, ref.shape[2] - 127, 128)]
            lane = lax.broadcasted_iota(jnp.int32, (width, 128), 1)
            spare = grad_qkv[slot, :, 3 * width - QKV_REST :]
            out_rest = grad_out[slot, :, width - OUT_REST :]
            columns = [jnp.sum(grad_gains[slot, n], axis=1, keepdims=True) for n in range(2)]
            rest = jnp.concatenate(
                [spare, out_rest] + columns
                + [jnp.zeros((width, 128 - QKV_REST - OUT_REST - 2), single)],
                axis=1,
            )
            blocks.append(rest)
            for n, block in enumerate(blocks):
                total[n * width : (n + 1) * width, :] = block.astype(total.dtype)
            used = len(blocks) * width
            total[used:, :] = jnp.zeros((total.shape[0] - used, 128), total.dtype)


def rotary_tables(length):
    frequency = 10000.0 ** (-np.arange(HALF, dtype=np.float64) / HALF)
    frequency = frequency.astype(np.float32)
    angles = np.arange(length, dtype=np.float32)[None, :] * frequency[:, None]
    return np.cos(angles).astype(np.float32), np.sin(angles).astype(np.float32)


def train(section, rows, raw, series_ids, median, scale, cotangent, own, other):
    count = raw.shape[0] // 2
    width, length = raw.shape[1:]
    heads = width // HEAD
    hidden = own[4].shape[1]
    place = jnp.stack([section, section * count]).astype(jnp.int32)
    cosine, sine = rotary_tables(length)
    operands = (raw, cotangent) + own + other + (jnp.asarray(cosine), jnp.asarray(sine))
    smem = pl.BlockSpec(memory_space=pltpu.SMEM)

    def whole(array):
        zeros = (0,) * len(array.shape)
        return pl.BlockSpec(
            array.shape, lambda i, *_: zeros, pipeline_mode=pl.Buffered(buffer_count=1)
        )

    placed_block = pl.BlockSpec((1, width, length), lambda i, place, ids: (place[1] + i, 0, 0))
    block = pl.BlockSpec((1, width, length), lambda i, *_: (i, 0, 0))
    shape = jax.ShapeDtypeStruct
    totals = (shape((rows, 128), single), shape((rows, 128), bfloat))
    pairs = length // TILE * (length // TILE + 1) // 2
    v = pltpu.VMEM
    scratch = [
        v((2, 2, width, 128), single),
        v((2, 3 * width, width), bfloat),
        v((2, width, width), bfloat),
        v((2, 2 * hidden, width), bfloat),
        v((2, width, hidden), bfloat),
        v((2, width, 3 * width), bfloat),
        v((2, width, width), bfloat),
        v((2, width, 2 * hidden), bfloat),
        v((2, hidden, width), bfloat),
        v((2, 2, width, 128), single),
        v((2, width, 3 * width), single),
        v((2, width, width), single),
        v((2, width, 2 * hidden), single),
        v((2, width, hidden), single),
        v((2, width, length), single),
        v((2, 1, length), single),
        v((2, width, length), bfloat),
        v((2, heads, HEAD, length), bfloat),
        v((2, heads, HEAD, length), bfloat),
        v((2, heads, 2 * HEAD, length), bfloat),
        v((heads, length, 2 * HEAD), bfloat),
        v((2, heads, pairs * TILE, TILE), bfloat),
        v((2, heads, HEAD, length), single),
        v((2, heads, 1, length), single),
        v((2, heads, HEAD, length), bfloat),
        v((2, width, length), single),
        v((2, 1, length), single),
        v((2, width, length), bfloat),
        v((2, 2 * hidden, length), single),
        v((2, hidden, length), bfloat),
        v((width, length), single),
        v((width, length), bfloat),
        v((2 * hidden, length), bfloat),
        v((width, length), bfloat),
        v((heads, 2 * HEAD, length), bfloat),
        v((heads, HEAD, length), single),
        v((heads, HEAD, length), single),
        v((heads, HEAD, length), single),
        v((3 * width, length), bfloat),
    ]
    return pl.pallas_call(
        functools.partial(train_kernel, heads, hidden),
        grid_spec=pltpu.PrefetchScalarGridSpec(
            num_scalar_prefetch=2,
            grid=(count,),
            in_specs=[smem, smem, placed_block, placed_block] + [whole(a) for a in operands[2:]],
            out_specs=[placed_block, placed_block, block, block] + [whole(t) for t in totals],
            scratch_shapes=scratch,
        ),
        out_shape=(
            shape(raw.shape, bfloat),
            shape(raw.shape, single),
            shape((count, width, length), bfloat),
            shape((count, width, length), bfloat),
        )
        + totals,
        compiler_params=pltpu.CompilerParams(vmem_limit_bytes=64 * 2**20 - 2**16),
    )(place, series_ids, median, scale, *operands)


def partner():
    return {"section": 1 - lax.axis_index("section")}


def meet(peers):
    barrier = pltpu.get_barrier_semaphore()
    for peer in peers:
        pl.semaphore_signal(barrier, inc=1, device_id=peer, device_id_type=MESH)
    pl.semaphore_wait(barrier, len(peers))


def swap_kernel(count, *refs):
    own, other, send, recv = refs[:count], refs[count : 2 * count], refs[-2], refs[-1]
    meet([partner()])
    copies = [
        pltpu.make_async_remote_copy(
            src_ref=own[n],
            dst_ref=other[n],
            send_sem=send.at[n],
            recv_sem=recv.at[n],
            device_id=partner(),
            device_id_type=MESH,
        )
        for n in range(count)
    ]
    for copy in copies:
        copy.start()
    for copy in copies:
        copy.wait()


def swap_weights(weights):
    count = len(weights)
    anywhere = pl.BlockSpec(memory_space=pl.ANY)
    return pl.pallas_call(
        functools.partial(swap_kernel, count),
        out_shape=tuple(jax.ShapeDtypeStruct(w.shape, w.dtype) for w in weights),
        in_specs=[anywhere] * count,
        out_specs=[anywhere] * count,
        scratch_shapes=[pltpu.SemaphoreType.DMA((count,)), pltpu.SemaphoreType.DMA((count,))],
        compiler_params=pltpu.CompilerParams(collective_id=0, has_side_effects=True),
    )(*weights)


def group_sizes(devices):
    sizes = []
    while devices > 1:
        size = 4 if devices % 4 == 0 else devices
        sizes.append(size)
        devices //= size
    return sizes


def reduce_kernel(
    sizes,
    own_total,
    other_total,
    sent_out,
    sent_grad,
    far_out,
    far_grad,
    grad_gains,
    grad_qkv,
    grad_out,
    grad_gate_up,
    grad_down,
    arrived,
    *scratch,
):
    count = len(sizes)
    parts = scratch[:count]
    slots = scratch[count : 2 * count]
    wholes = scratch[2 * count : 3 * count]
    last, swap_send, swap_recv, sum_send, sum_recv, gather_send, gather_recv = scratch[3 * count :]
    me = lax.axis_index("dp")
    places, groups = [], []
    stride = 1
    for size in sizes:
        place = lax.rem(lax.div(me, stride), size)
        peers = []
        for turn in range(1, size):
            other = lax.rem(place + turn, size)
            peers.append((other, {"dp": me + (other - place) * stride}))
        places.append(place)
        groups.append(peers)
        stride *= size
    meet([partner()] + [device for peers in groups for _, device in peers])

    def copy(source, target, send, recv, device):
        c = pltpu.make_async_remote_copy(
            src_ref=source,
            dst_ref=target,
            send_sem=send,
            recv_sem=recv,
            device_id=device,
            device_id_type=MESH,
        )
        c.start()
        return c

    near = copy(other_total, arrived, swap_send.at[0], swap_recv.at[0], partner())
    far = [
        copy(sent_out, far_out, swap_send.at[1], swap_recv.at[1], partner()),
        copy(sent_grad, far_grad, swap_send.at[2], swap_recv.at[2], partner()),
    ]
    near.wait()
    parts[0][...] = (own_total[...] + arrived[...].astype(single)).astype(bfloat)
    first = 0
    starts = []
    for n, size in enumerate(sizes):
        chunk = parts[n].shape[0] // size
        copies = []
        for turn, (other, device) in enumerate(groups[n]):
            copies.append(
                copy(
                    parts[n].at[pl.ds(pl.multiple_of(other * chunk, 16), chunk)],
                    slots[n].at[turn],
                    sum_send.at[first + turn],
                    sum_recv.at[first + turn],
                    device,
                )
            )
        total = parts[n][pl.ds(pl.multiple_of(places[n] * chunk, 16), chunk), :].astype(single)
        for turn, c in enumerate(copies):
            c.wait()
            total = total + slots[n][turn].astype(single)
        target = parts[n + 1] if n + 1 < count else last
        target[...] = total.astype(bfloat)
        starts.append(first)
        first += size - 1
    source = last
    for n in reversed(range(count)):
        chunk = parts[n].shape[0] // sizes[n]
        mine = pl.ds(pl.multiple_of(places[n] * chunk, 16), chunk)
        copies = []
        for turn, (_, device) in enumerate(groups[n]):
            k = starts[n] + turn
            copies.append(
                copy(source, wholes[n].at[mine], gather_send.at[k], gather_recv.at[k], device)
            )
        wholes[n][mine, :] = source[...]
        for c in copies:
            c.wait()
        source = wholes[n]
    width = grad_qkv.shape[0]
    block = 0
    for ref in (grad_gate_up, grad_down, grad_qkv, grad_out):
        for n in range(0, ref.shape[1] - 127, 128):
            ref[:, n : n + 128] = source[block * width : (block + 1) * width, :].astype(single)
            block += 1
    rest = source[block * width : (block + 1) * width, :].astype(single)
    grad_qkv[:, 3 * width - QKV_REST :] = rest[:, :QKV_REST]
    grad_out[:, width - OUT_REST :] = rest[:, QKV_REST : QKV_REST + OUT_REST]
    grad_gains[...] = rest.T[QKV_REST + OUT_REST : QKV_REST + OUT_REST + 2, :]
    for c in far:
        c.wait()


def reduce(devices, own_total, other_total, sent_out, sent_grad, width, hidden):
    sizes = group_sizes(devices)
    rows = own_total.shape[0]
    v = pltpu.VMEM
    shape = jax.ShapeDtypeStruct
    parts, slots, left = [], [], rows
    for size in sizes:
        parts.append(v((left, 128), bfloat))
        left //= size
        slots.append(v((size - 1, left, 128), bfloat))
    links = sum(size - 1 for size in sizes)
    dma = pltpu.SemaphoreType.DMA
    anywhere = pl.BlockSpec(memory_space=pl.ANY)
    vmem = pl.BlockSpec(memory_space=pltpu.VMEM)
    return pl.pallas_call(
        functools.partial(reduce_kernel, sizes),
        out_shape=(
            shape(sent_out.shape, bfloat),
            shape(sent_grad.shape, bfloat),
            shape((2, width), single),
            shape((width, 3 * width), single),
            shape((width, width), single),
            shape((width, 2 * hidden), single),
            shape((width, hidden), single),
        ),
        in_specs=[vmem, vmem, anywhere, anywhere],
        out_specs=[anywhere, anywhere] + [vmem] * 5,
        scratch_shapes=[v((rows, 128), bfloat)]
        + parts
        + slots
        + parts
        + [v((left, 128), bfloat), dma((3,)), dma((3,))]
        + [dma((links,))] * 4,
        compiler_params=pltpu.CompilerParams(
            collective_id=1, has_side_effects=True, vmem_limit_bytes=40 * 2**20
        ),
    )(own_total, other_total, sent_out, sent_grad)


def on_device(
    devices,
    raw,
    series_ids,
    median,
    scale,
    cotangent,
    norm_gains,
    qkv_weight,
    out_weight,
    gate_up_weight,
    down_weight,
):
    section = lax.axis_index("section")
    turned = lambda a: jnp.swapaxes(a, -1, -2)
    count = raw.shape[0] // 2
    width, hidden = raw.shape[2], down_weight.shape[1]
    own = (norm_gains[0], qkv_weight[0], out_weight[0], gate_up_weight[0], turned(down_weight[0]))
    other = swap_weights(own)
    blocks = 14
    rows = -(-blocks * width // (16 * devices)) * 16 * devices
    kept_out, kept_grad, sent_out, sent_grad, own_total, other_total = train(
        section, rows, turned(raw), series_ids, median, scale, turned(cotangent), own, other
    )
    far_out, far_grad, gain, qkv, out, gate_up, down = reduce(
        devices, own_total, other_total, sent_out, sent_grad, width, hidden
    )
    place = ((1 - section) * count, 0, 0)
    layer_outputs = lax.dynamic_update_slice(kept_out, far_out, place)
    input_grads = lax.dynamic_update_slice(kept_grad, far_grad.astype(single), place)
    return (
        turned(layer_outputs)[None],
        turned(input_grads)[None],
        gain[None],
        qkv[None],
        out[None],
        gate_up[None],
        turned(down)[None],
    )


def solution(mesh):
    placed = (
        P("dp", None, None),
        P("dp"),
        P(),
        P(),
        P("dp", None, None),
        P("section", None, None),
        P("section", None, None),
        P("section", None, None),
        P("section", None, None),
        P("section", None, None),
    )
    return jax.shard_map(
        functools.partial(on_device, mesh.shape["dp"]),
        mesh=mesh,
        in_specs=placed,
        out_specs=(
            P("section", "dp", None, None),
            P("section", "dp", None, None),
            P("section", None, None),
            P("section", None, None),
            P("section", None, None),
            P("section", None, None),
            P("section", None, None),
        ),
        check_vma=False,
    )
```

time: 2570 us -> 234 us (0.09)
  matrix products: 819 us -> 0 us
  waiting for transfers between devices: 607 us -> 0 us
  other arithmetic: 505 us -> 0.9 us
  blocking collectives: 364 us -> 0 us
  Pallas kernels: 0 us -> 222 us
  local copies, waits for them, and re-layouts: 152 us -> 9.88 us
  loops' own time: 56.8 us -> 0 us
  starting transfers between devices: 30.5 us -> 0 us
    dot_general x236 -> x0, matrix products: 819 us -> none  [the longest x18 178 us: layer_backward(): jnp.einsum('qhe,khe->hqk', grad_attended[first_row:end_row], values[:end_...]
    psum x9 -> x0, waiting for transfers between devices: 607 us -> none  [backward_tick(): lax.psum((gain_grad, qkv_grad, out_grad, gu_grad, down_grad), 'dp')]
    psum x9 -> x0, blocking collectives: 364 us -> none  [backward_tick(): lax.psum((gain_grad, qkv_grad, out_grad, gu_grad, down_grad), 'dp')]
    convert_element_type x36 -> x0, other arithmetic: 224 us -> none  [the longest x18 223 us: layer_backward(): grad_scores = (probabilities * (grad_probs - centre)).astype(bfloat)]
    pallas_call x0 -> x3, Pallas kernels: none -> 222 us  [the longest x1 189 us: train(): pl.pallas_call(functools.partial(train_kernel, heads, hidden), grid_spec=...]
    reduce_sum x27 -> x0, other arithmetic: 106 us -> none  [the longest x18 95.1 us: layer_forward(): row_total = jnp.sum(exponent, axis=-1, keepdims=True)]
    dynamic_update_slice x63 -> x1, other arithmetic: 90.4 us -> 0.31 us  [on_device(): lax.dynamic_update_slice(kept_grad, far_grad.astype(single), place)]
    dynamic_slice x63 -> x0, local copies, waits for them, and re-layouts: 66.9 us -> none  [the longest x45 50.3 us: backward_tick(): lax.dynamic_index_in_dim(member, which, 0, keepdims=False)]
  transfers between devices with their start and end apart: 27 -> 0, of which waited for: 9 -> 0; matrix products, arithmetic and copies ran while one was open for 4% -> 0% of each run, Pallas kernels for 0% -> 0%
where the time goes in v1:
time: 234 us; the launch traced here: 233 us
  Pallas kernels  222 us (95%)
  local copies, waits for them, and re-layouts  9.88 us (4%)
    pallas_call x1, Pallas kernels, train(): pl.pallas_call(functools.partial(train_kernel, heads, hidden), grid_spec=...  189 us
    pallas_call x1, Pallas kernels, reduce(): pl.pallas_call(functools.partial(reduce_kernel, sizes), out_shape=(shape(...  30.1 us
    unnamed x17, local copies, waits for them, and re-layouts  8.78 us

profile of v1, /device:TPU:0, one launch (start us, length us, event | category | flops | bytes accessed | tf_op | source)
XLA Modules:
  0.0 233.2 jit_solution(7480421638067904819)
XLA Ops:
  0.6 0.6 pad_add_fusion.place
  1.2 2.5 %shard_map.171 = (f32[2,144]{1,0:T(2,128)}, bf16[144,432]{1,0:T(8,128)(2,1)}, bf16[144,144]{1,0:T(8,128)(2,1)}, bf16[144,768]{1,0:T(8,128)(2,1)}, bf16[144,384]{1,0:T(8,128)(2,1)}) custom-call(f32[2,144]{1,0:T(2,128)} %bitcast.39, bf16[144,432]{1,0:T(8,128)(2,1)} %bitcast.33, bf16[144,144]{1,0:T(8,128)(2,1)} %bitcast.37, bf16[144,768]{1,0:T(8,128)(2,1)} %bitcast.31, ...), custom_call_target="tpu_custom_call" | custom-call | tf_op jit(solution)/shard_map/pallas_call | solution.py:549
  3.7 189.2 %shard_map.172 = (bf16[8,144,1024]{2,1,0:T(8,128)(2,1)}, f32[8,144,1024]{2,1,0:T(8,128)}, bf16[4,144,1024]{2,1,0:T(8,128)(2,1)}, bf16[4,144,1024]{2,1,0:T(8,128)...) custom-call(s32[2]{0:T(128)} %pad_add_fusion.place, s32[8]{0:T(128)} %series_ids.1, f32[128]{0:T(128)} %median.1, ...), custom_call_target="tpu_custom_call" | custom-call | tf_op jit(solution)/shard_map/pallas_call | solution.py:495
  192.9 0.0 copy-start
  192.9 1.3 copy-done
  194.1 0.0 copy-start.1
  194.1 1.3 copy-done.1
  195.4 0.0 copy-start.2
  195.4 1.2 copy-done.2
  196.6 0.0 copy-start.3
  196.6 1.0 copy-done.3
  197.7 0.0 copy-start.4
  197.7 30.1 %shard_map.173 = (bf16[4,144,1024]{2,1,0:T(8,128)(2,1)S(1)}, bf16[4,144,1024]{2,1,0:T(8,128)(2,1)S(1)}, f32[2,144]{1,0:T(2,128)S(1)}, f32[144,432]{1,0:T(8,128)S...) custom-call(f32[2048,128]{1,0:T(8,128)S(1)} %copy-done.2, ...), custom_call_target="tpu_custom_call" | custom-call | tf_op jit(solution)/shard_map/pallas_call | solution.py:687
  227.8 1.1 constant_dynamic-update-slice_fusion
  228.9 0.0 copy-done.4
  228.9 0.3 convert_dynamic-update-slice_fusion
  229.2 0.0 copy-start.5
  229.2 0.6 copy.26
  229.8 1.3 copy.27
  231.1 0.7 copy.28
  231.7 0.8 copy.29
  232.5 0.7 copy.30
  233.2 0.0 copy-done.5
Async XLA Ops:
  192.9 1.3 copy-start
  194.1 1.3 copy-start.1
  195.4 1.2 copy-start.2
  196.6 1.0 copy-start.3
  197.7 31.2 %copy-start.4 = (f32[8,144,1024]{2,1,0:T(8,128)S(1)}, f32[8,144,1024]{2,1,0:T(8,128)}, u32[]{:S(2)}) copy-start(f32[8,144,1024]{2,1,0:T(8,128)} %get-tuple-element.36) | copy-start | bytes 14155780
  229.2 4.0 %copy-start.5 = (f32[8,144,1024]{2,1,0:T(8,128)}, f32[8,144,1024]{2,1,0:T(8,128)S(1)}, u32[]{:S(2)}) copy-start(f32[8,144,1024]{2,1,0:T(8,128)S(1)} %convert_dynamic-update-slice_fusion) | copy-start | bytes 14155780

commit v2 on v1

--- a/solution.py
+++ b/solution.py
@@ -52,6 +52,15 @@
 
 def tile_start(j):
     return j * (j + 1) // 2 * TILE
+
+
+def lanes(tiles):
+    full = [(j, k) for j in range(tiles) for k in range(j + 1)]
+    sides = [[(side, j, k) for j, k in full] for side in range(2)]
+    for j in reversed(range(tiles)):
+        side = min(sides, key=len)
+        side += [(2, j, k) for k in range(j + 1)]
+    return list(zip(*sides))
 
 
 def train_kernel(
@@ -120,6 +129,7 @@
     grad_k,
     grad_v,
     grad_proj,
+    flipped,
 ):
     step = pl.program_id(0)
     section = place[0]
@@ -137,7 +147,7 @@
             ref[...] = jnp.zeros_like(ref)
         row = lax.broadcasted_iota(jnp.int32, (2, heads, HEAD, length), 2)
         values[:, :, HEAD:, :] = jnp.where(row < 2, 1.0, 0.0).astype(bfloat)
-        flipped = lambda w: w.astype(single).T.astype(bfloat)
+        turned = lambda w: w.astype(single).T.astype(bfloat)
         for l, (gain, qkv, out, both, down) in (
             (section, (own_gains, own_qkv, own_out, own_gate_up, own_down_t)),
             (1 - section, (other_gains, other_qkv, other_out, other_gate_up, other_down_t)),
@@ -146,13 +156,13 @@
                 row = jnp.broadcast_to(gain[part : part + 1, :], (128, width))
                 gains[l, part] = row.T
             qkv_w[l] = qkv[...]
-            qkv_t[l] = flipped(qkv[...])
+            qkv_t[l] = turned(qkv[...])
             out_w[l] = out[...]
-            out_t[l] = flipped(out[...])
+            out_t[l] = turned(out[...])
             gate_up_w[l] = both[...]
-            gate_up_t[l] = flipped(both[...])
+            gate_up_t[l] = turned(both[...])
             down_t[l] = down[...]
-            down_w[l] = flipped(down[...])
+            down_w[l] = turned(down[...])
 
     def gain_of(l, part):
         return jnp.concatenate([gains[l, part]] * (TILE // 128), axis=1)
@@ -202,44 +212,43 @@
 
         @pl.when(small)
         def _():
-            group = 3
+            pairs = lanes(tiles)
             ahead = 3
 
-            def some(hh, carry):
-                work = [
-                    (hh * group + g, j, k)
-                    for g in range(group)
-                    for j in range(tiles)
-                    for k in range(j + 1)
-                ]
+            def some(three, carry):
                 scores = {}
 
-                def score(n):
-                    h, j, k = work[n]
-                    scores[n] = dot(
-                        rows_major[h, k * TILE : (k + 1) * TILE, :HEAD],
-                        queries[l, h, :, j * TILE : (j + 1) * TILE],
-                    )
-
-                for n in range(ahead):
-                    score(n)
-                total = None
-                for n, (h, j, k) in enumerate(work):
-                    if n + ahead < len(work):
-                        score(n + ahead)
-                    e = jnp.exp2(scores.pop(n))
-                    if k == j:
-                        e = jnp.where(causal(e), e, 0.0)
-                    e = e.astype(bfloat)
-                    first = tile_start(j) + k * TILE
-                    exponents[l, h, first : first + TILE, :] = e
-                    part = dot(values[l, h, :, k * TILE : (k + 1) * TILE], e)
-                    total = part if k == 0 else total + part
-                    if k == j:
-                        finish(h, j, total)
+                def score(m):
+                    for side, (g, j, k) in enumerate(pairs[m]):
+                        scores[m, side] = dot(
+                            rows_major[three * 3 + g, k * TILE : (k + 1) * TILE, :HEAD],
+                            queries[l, three * 3 + g, :, j * TILE : (j + 1) * TILE],
+                        )
+
+                for m in range(ahead):
+                    score(m)
+                totals = {}
+                for m, pair in enumerate(pairs):
+                    if m + ahead < len(pairs):
+                        score(m + ahead)
+                    ready = []
+                    for side, (g, j, k) in enumerate(pair):
+                        e = jnp.exp2(scores.pop((m, side)))
+                        if k == j:
+                            e = jnp.where(causal(e), e, 0.0)
+                        e = e.astype(bfloat)
+                        first = tile_start(j) + k * TILE
+                        exponents[l, three * 3 + g, first : first + TILE, :] = e.T
+                        ready.append(e)
+                    for side, (g, j, k) in enumerate(pair):
+                        h = three * 3 + g
+                        part = dot(values[l, h, :, k * TILE : (k + 1) * TILE], ready[side])
+                        totals[g, j] = totals[g, j] + part if k else part
+                        if k == j:
+                            finish(h, j, totals.pop((g, j)))
                 return carry
 
-            lax.fori_loop(0, heads // group, some, 0)
+            lax.fori_loop(0, heads // 3, some, 0)
 
         @pl.when(jnp.logical_not(small))
         def _():
@@ -252,7 +261,9 @@
                     columns = lax.broadcasted_iota(jnp.int32, score.shape, 1) + j * TILE
                     score = jnp.where(rows <= columns, score, -1e30)
                     e = jnp.exp2(score - jnp.max(score, axis=0, keepdims=True)).astype(bfloat)
-                    exponents[l, h, tile_start(j) : tile_start(j) + count, :] = e
+                    for k in range(j + 1):
+                        first = tile_start(j) + k * TILE
+                        exponents[l, h, first : first + TILE, :] = e[k * TILE : (k + 1) * TILE].T
                     finish(h, j, dot(values[l, h, :, :count], e))
                 return carry
 
@@ -326,51 +337,67 @@
         grad_out[slot] += dot_nt(attended[l].reshape(width, length), grad_res_low[...])
 
         for h in range(heads):
-            rows_major[h] = values[l, h].astype(single).T.astype(bfloat)
-
-        group = 3
-        ahead = 3
-
-        def some(hh, carry):
-            work = [
-                (g, j, k) for g in range(group) for j in range(tiles) for k in range(j + 1)
-            ]
-            products = {}
-
-            def product(n):
-                g, j, k = work[n]
-                products[n] = dot(
-                    rows_major[hh * group + g, k * TILE : (k + 1) * TILE, :],
-                    grad_att[hh * group + g, :, j * TILE : (j + 1) * TILE],
-                )
-
-            for n in range(ahead):
-                product(n)
-            sums = {}
-
-            def add(key, value):
+            rows_major[h] = grad_att[h].astype(single).T.astype(bfloat)
+
+        pairs = lanes(tiles)
+        ahead = 2
+        half = TILE // 2
+
+        def some(three, carry):
+            products, held, sums = {}, {}, {}
+
+            def product(m, part):
+                if m < len(pairs):
+                    for side, (g, j, k) in enumerate(pairs[m]):
+                        first = j * TILE + part * half
+                        products[m, side, part] = dot(
+                            rows_major[three * 3 + g, first : first + half, :],
+                            values[l, three * 3 + g, :, k * TILE : (k + 1) * TILE],
+                        )
+
+            def add(name, index, side, g, value):
+                key = name, g, index, side
                 sums[key] = sums[key] + value if key in sums else value
 
-            for n, (g, j, k) in enumerate(work):
-                h = hh * group + g
-                if n + ahead < len(work):
-                    product(n + ahead)
-                first = tile_start(j) + k * TILE
-                e = exponents[l, h, first : first + TILE, :]
-                grad_score = e * products.pop(n).astype(bfloat)
-                js, ks = slice(j * TILE, (j + 1) * TILE), slice(k * TILE, (k + 1) * TILE)
-                add(("q", j), dot(keys[l, h, :, ks], grad_score))
-                add(("k", k), dot_nt(queries[l, h, :, js], grad_score))
-                add(("v", k), dot_nt(grad_att[h, :HEAD, js], e))
-                if (j, k) == (tiles - 1, tiles - 1):
+            for m in range(ahead):
+                product(m, 0)
+                product(m, 1)
+            for m in range(len(pairs) + 1):
+                now = pairs[m] if m < len(pairs) else ()
+                before = pairs[m - 1] if m > 0 else ()
+                product(m + ahead, 0)
+                exps = []
+                for side, (g, j, k) in enumerate(now):
+                    first = tile_start(j) + k * TILE
+                    e = exponents[l, three * 3 + g, first : first + TILE, :]
+                    parts = [
+                        e[p * half : (p + 1) * half] * products.pop((m, side, p)).astype(bfloat)
+                        for p in range(2)
+                    ]
+                    grad_score = jnp.concatenate(parts, axis=0)
+                    flipped[m % 2, side] = grad_score.T
+                    held[m, side] = grad_score
+                    exps.append(e)
+                for side, (g, j, k) in enumerate(now):
+                    js = slice(j * TILE, (j + 1) * TILE)
+                    add("v", k, side, g, dot(grad_att[three * 3 + g, :HEAD, js], exps[side]))
+                product(m + ahead, 1)
+                for side, (g, j, k) in enumerate(before):
+                    js = slice(j * TILE, (j + 1) * TILE)
+                    grad_score = held.pop((m - 1, side))
+                    add("k", k, side, g, dot(queries[l, three * 3 + g, :, js], grad_score))
+                for side, (g, j, k) in enumerate(before):
+                    ks = slice(k * TILE, (k + 1) * TILE)
+                    turned = flipped[(m - 1) % 2, side]
+                    add("q", j, side, g, dot(keys[l, three * 3 + g, :, ks], turned))
+            for g in range(3):
+                for name, ref in (("q", grad_q), ("k", grad_k), ("v", grad_v)):
                     for t in range(tiles):
-                        ts = slice(t * TILE, (t + 1) * TILE)
-                        grad_q[h, :, ts] = sums.pop(("q", t))
-                        grad_k[h, :, ts] = sums.pop(("k", t))
-                        grad_v[h, :, ts] = sums.pop(("v", t))
+                        found = [sums[name, g, t, n] for n in range(2) if (name, g, t, n) in sums]
+                        ref[three * 3 + g, :, t * TILE : (t + 1) * TILE] = sum(found[1:], found[0])
             return carry
 
-        lax.fori_loop(0, heads // group, some, 0)
+        lax.fori_loop(0, heads // 3, some, 0)
 
         for c in range(tiles):
             cs = slice(c * TILE, (c + 1) * TILE)
@@ -491,6 +518,7 @@
         v((heads, HEAD, length), single),
         v((heads, HEAD, length), single),
         v((3 * width, length), bfloat),
+        v((2, 2, TILE, TILE), bfloat),
     ]
     return pl.pallas_call(
         functools.partial(train_kernel, heads, hidden),

time: 234 us -> 209 us (0.89)
  Pallas kernels: 222 us -> 197 us
    pallas_call x1, Pallas kernels: 189 us -> 165 us  [train(): pl.pallas_call(functools.partial(train_kernel, heads, hidden), grid_spec=...]
where the time goes in v2:
time: 209 us
  Pallas kernels  197 us (94%)
  local copies, waits for them, and re-layouts  9.88 us (5%)
    pallas_call x1, Pallas kernels, train(): pl.pallas_call(functools.partial(train_kernel, heads, hidden), grid_spec=...  165 us
    pallas_call x1, Pallas kernels, reduce(): pl.pallas_call(functools.partial(reduce_kernel, sizes), out_shape=(shape(...  30 us
    unnamed x17, local copies, waits for them, and re-layouts  8.78 us

profile of v2, /device:TPU:0, one launch (start us, length us, event | category | flops | bytes accessed | tf_op | source)
XLA Modules:
  0.0 208.7 jit_solution(15078979097210619573)
XLA Ops:
  0.6 0.6 pad_add_fusion.place
  1.2 2.5 %shard_map.171 = (f32[2,144]{1,0:T(2,128)}, bf16[144,432]{1,0:T(8,128)(2,1)}, bf16[144,144]{1,0:T(8,128)(2,1)}, bf16[144,768]{1,0:T(8,128)(2,1)}, bf16[144,384]{1,0:T(8,128)(2,1)}) custom-call(f32[2,144]{1,0:T(2,128)} %bitcast.39, bf16[144,432]{1,0:T(8,128)(2,1)} %bitcast.33, bf16[144,144]{1,0:T(8,128)(2,1)} %bitcast.37, bf16[144,768]{1,0:T(8,128)(2,1)} %bitcast.31, ...), custom_call_target="tpu_custom_call" | custom-call | tf_op jit(solution)/shard_map/pallas_call | solution.py:577
  3.7 164.7 %shard_map.172 = (bf16[8,144,1024]{2,1,0:T(8,128)(2,1)}, f32[8,144,1024]{2,1,0:T(8,128)}, bf16[4,144,1024]{2,1,0:T(8,128)(2,1)}, bf16[4,144,1024]{2,1,0:T(8,128)...) custom-call(s32[2]{0:T(128)} %pad_add_fusion.place, s32[8]{0:T(128)} %series_ids.1, f32[128]{0:T(128)} %median.1, ...), custom_call_target="tpu_custom_call" | custom-call | tf_op jit(solution)/shard_map/pallas_call | solution.py:523
  168.4 0.0 copy-start
  168.5 1.3 copy-done
  169.7 0.0 copy-start.1
  169.7 1.3 copy-done.1
  171.0 0.0 copy-start.2
  171.0 1.2 copy-done.2
  172.2 0.0 copy-start.3
  172.2 1.0 copy-done.3
  173.3 0.0 copy-start.4
  173.3 30.0 %shard_map.173 = (bf16[4,144,1024]{2,1,0:T(8,128)(2,1)S(1)}, bf16[4,144,1024]{2,1,0:T(8,128)(2,1)S(1)}, f32[2,144]{1,0:T(2,128)S(1)}, f32[144,432]{1,0:T(8,128)S...) custom-call(f32[2048,128]{1,0:T(8,128)S(1)} %copy-done.2, ...), custom_call_target="tpu_custom_call" | custom-call | tf_op jit(solution)/shard_map/pallas_call | solution.py:715
  203.3 1.1 constant_dynamic-update-slice_fusion
  204.4 0.0 copy-done.4
  204.4 0.3 convert_dynamic-update-slice_fusion
  204.7 0.0 copy-start.5
  204.7 0.6 copy.26
  205.3 1.3 copy.27
  206.6 0.7 copy.28
  207.2 0.8 copy.29
  208.0 0.7 copy.30
  208.7 0.0 copy-done.5
Async XLA Ops:
  168.4 1.3 copy-start
  169.7 1.3 copy-start.1
  171.0 1.2 copy-start.2
  172.2 1.0 copy-start.3
  173.3 31.1 %copy-start.4 = (f32[8,144,1024]{2,1,0:T(8,128)S(1)}, f32[8,144,1024]{2,1,0:T(8,128)}, u32[]{:S(2)}) copy-start(f32[8,144,1024]{2,1,0:T(8,128)} %get-tuple-element.36) | copy-start | bytes 14155780
  204.7 4.0 %copy-start.5 = (f32[8,144,1024]{2,1,0:T(8,128)}, f32[8,144,1024]{2,1,0:T(8,128)S(1)}, u32[]{:S(2)}) copy-start(f32[8,144,1024]{2,1,0:T(8,128)S(1)} %convert_dynamic-update-slice_fusion) | copy-start | bytes 14155780

commit v3 on v2

--- a/solution.py
+++ b/solution.py
@@ -12,6 +12,7 @@
 HEAD = 16
 HALF = HEAD // 2
 TILE = 256
+CHUNK = 512
 EPSILON = 1e-06
 LOG2E = math.log2(math.e)
 QKV_REST = 48
@@ -82,8 +83,7 @@
     other_out,
     other_gate_up,
     other_down_t,
-    cosine,
-    sine,
+    tables,
     kept_out,
     kept_grad,
     sent_out,
@@ -130,6 +130,7 @@
     grad_v,
     grad_proj,
     flipped,
+    grad_inputs,
 ):
     step = pl.program_id(0)
     section = place[0]
@@ -139,7 +140,7 @@
     inverse_spread = 1.0 / scale[number]
     width, length = inputs.shape[1:]
     tiles = length // TILE
-    query_factor = HEAD**-0.5 * LOG2E
+    chunks = [slice(n, n + CHUNK) for n in range(0, length, CHUNK)]
 
     @pl.when(step == 0)
     def _():
@@ -165,40 +166,44 @@
             down_w[l] = turned(down[...])
 
     def gain_of(l, part):
-        return jnp.concatenate([gains[l, part]] * (TILE // 128), axis=1)
+        return jnp.concatenate([gains[l, part]] * (CHUNK // 128), axis=1)
 
     inputs[0] = (raw[0].astype(single) - centre) * inverse_spread
     grad[...] = cotangent[0].astype(single)
 
-    def rotated(block, cs, sign):
+    def rotated(block, cos, sin):
         a, b = block[:, :HALF], block[:, HALF:]
-        cos, sin = cosine[:, cs], sine[:, cs] * sign
         return jnp.concatenate([a * cos - b * sin, b * cos + a * sin], axis=1)
 
+    head_rows = lax.broadcasted_iota(jnp.int32, (HEAD, width), 0)
+    head_columns = lax.broadcasted_iota(jnp.int32, (HEAD, width), 1)
+    of_head = jnp.where(
+        (head_columns >= head_rows * HEAD) & (head_columns < (head_rows + 1) * HEAD), 1.0, 0.0
+    ).astype(bfloat)
+
     def forward(l, carry):
-        largest = jnp.zeros((1, 1, TILE), single)
-        largest_q = jnp.zeros((heads, 1, TILE), single)
-        largest_k = jnp.zeros((heads, 1, TILE), single)
-        for c in range(tiles):
-            cs = slice(c * TILE, (c + 1) * TILE)
+        largest_q = jnp.zeros((HEAD, CHUNK), single)
+        largest_k = jnp.zeros((HEAD, CHUNK), single)
+        for cs in chunks:
             u = inputs[l, :, cs]
             inv = rms_scale(u)
             inverse1[l, :, cs] = inv
             low = (u * inv * gain_of(l, 0)).astype(bfloat)
             normed[l, :, cs] = low
-            projected = dot(qkv_t[l], low).reshape(3 * heads, HEAD, TILE)
-            q = (rotated(projected[:heads], cs, 1.0) * query_factor).astype(bfloat)
-            k = rotated(projected[heads : 2 * heads], cs, 1.0)
-            queries[l, :, :, cs] = q
+            projected = dot(qkv_t[l], low).reshape(3 * heads, HEAD, CHUNK)
+            q = rotated(projected[:heads], tables[2, :, cs], tables[3, :, cs])
+            k = rotated(projected[heads : 2 * heads], tables[0, :, cs], tables[1, :, cs])
+            queries[l, :, :, cs] = q.astype(bfloat)
             keys[l, :, :, cs] = k.astype(bfloat)
             values[l, :, :HEAD, cs] = projected[2 * heads :].astype(bfloat)
             for h in range(heads):
                 rows_major[h, cs, :HEAD] = k[h].T.astype(bfloat)
-            q32 = q.astype(single)
-            k32 = k.astype(bfloat).astype(single)
-            largest_q = jnp.maximum(largest_q, jnp.sum(q32 * q32, axis=1, keepdims=True))
-            largest_k = jnp.maximum(largest_k, jnp.sum(k32 * k32, axis=1, keepdims=True))
-        bound = jnp.max(jnp.max(largest_q, axis=2) * jnp.max(largest_k, axis=2))
+            squares = lambda v: dot(of_head, (v * v).astype(bfloat).reshape(width, CHUNK))
+            largest_q = jnp.maximum(largest_q, squares(q))
+            largest_k = jnp.maximum(largest_k, squares(k))
+        bound = jnp.max(
+            jnp.max(largest_q, axis=1, keepdims=True) * jnp.max(largest_k, axis=1, keepdims=True)
+        )
 
         def finish(h, j, total):
             js = slice(j * TILE, (j + 1) * TILE)
@@ -269,34 +274,23 @@
 
             lax.fori_loop(0, heads, one, 0)
 
-        for c in range(tiles):
-            cs = slice(c * TILE, (c + 1) * TILE)
-            res = inputs[l, :, cs] + dot(out_t[l], attended[l, :, :, cs].reshape(width, TILE))
+        for cs in chunks:
+            res = inputs[l, :, cs] + dot(out_t[l], attended[l, :, :, cs].reshape(width, CHUNK))
             residual[l, :, cs] = res
             inv = rms_scale(res)
             inverse2[l, :, cs] = inv
             low = (res * inv * gain_of(l, 1)).astype(bfloat)
             mid[l, :, cs] = low
             both = dot(gate_up_t[l], low)
-            gate_up[l, :, cs] = both
             gate, up = both[:hidden], both[hidden:]
-            act = (gate * jax.nn.sigmoid(gate) * up).astype(bfloat)
+            sig = 0.5 * jnp.tanh(0.5 * gate) + 0.5
+            swish = gate * sig
+            gate_up[l, :hidden, cs] = up * (sig + swish * (1.0 - sig))
+            gate_up[l, hidden:, cs] = swish
+            act = (swish * up).astype(bfloat)
             activated[l, :, cs] = act
             result = res + dot(down_t[l], act)
-            low = result.astype(bfloat)
-
-            @pl.when(l == section)
-            def _():
-                kept_out[0, :, cs] = low
-
-            @pl.when(l != section)
-            def _():
-                sent_out[0, :, cs] = low
-
-            @pl.when(l == 0)
-            def _():
-                inputs[1, :, cs] = low.astype(single)
-
+            inputs[l + 1, :, cs] = result.astype(bfloat).astype(single)
         return carry
 
     lax.fori_loop(0, 2, forward, 0)
@@ -304,18 +298,14 @@
     def backward(turn, carry):
         l = 1 - turn
         slot = lax.rem(l + section, 2)
-        for c in range(tiles):
-            cs = slice(c * TILE, (c + 1) * TILE)
+        for cs in chunks:
             g = grad[:, cs]
             low = g.astype(bfloat)
             grad_low[:, cs] = low
             grad_act = dot(down_w[l], low)
-            gate, up = gate_up[l, :hidden, cs], gate_up[l, hidden:, cs]
-            sig = jax.nn.sigmoid(gate)
-            inner = grad_act * sig
-            grad_gate = inner * up * (1.0 + gate * (1.0 - sig))
-            grad_up = inner * gate
-            pre = jnp.concatenate([grad_gate, grad_up], axis=0).astype(bfloat)
+            pre = jnp.concatenate(
+                [grad_act * gate_up[l, :hidden, cs], grad_act * gate_up[l, hidden:, cs]], axis=0
+            ).astype(bfloat)
             grad_pre[:, cs] = pre
             grad_mid = dot(gate_up_w[l], pre)
             res, inv = residual[l, :, cs], inverse2[l, :, cs]
@@ -325,13 +315,14 @@
             grad[:, cs] = grad_res
             low = grad_res.astype(bfloat)
             grad_res_low[:, cs] = low
-            back = dot(out_w[l], low).astype(bfloat).astype(single).reshape(heads, HEAD, TILE)
+            back = dot(out_w[l], low).astype(bfloat).astype(single).reshape(heads, HEAD, CHUNK)
             inverse = reciprocal[l, :, :, cs]
             mean = jnp.sum(back * attended32[l, :, :, cs], axis=1, keepdims=True) * -inverse
             coarse = mean.astype(bfloat).astype(single)
-            row = lax.broadcasted_iota(jnp.int32, (heads, HEAD, TILE), 1)
+            row = lax.broadcasted_iota(jnp.int32, (heads, HALF, CHUNK), 1)
             extra = jnp.where(row == 0, coarse, jnp.where(row == 1, mean - coarse, 0.0))
-            grad_att[:, :, cs] = jnp.concatenate([back * inverse, extra], axis=1).astype(bfloat)
+            rest = jnp.zeros((heads, HALF, CHUNK), single)
+            grad_att[:, :, cs] = jnp.concatenate([back * inverse, extra, rest], axis=1).astype(bfloat)
         grad_down[slot] += dot_nt(grad_low[...], activated[l])
         grad_gate_up[slot] += dot_nt(mid[l], grad_pre[...])
         grad_out[slot] += dot_nt(attended[l].reshape(width, length), grad_res_low[...])
@@ -399,12 +390,11 @@
 
         lax.fori_loop(0, heads // 3, some, 0)
 
-        for c in range(tiles):
-            cs = slice(c * TILE, (c + 1) * TILE)
-            dq = rotated(grad_q[:, :, cs] * HEAD**-0.5, cs, -1.0)
-            dk = rotated(grad_k[:, :, cs] * (1.0 / LOG2E), cs, -1.0)
+        for cs in chunks:
+            dq = rotated(grad_q[:, :, cs], tables[4, :, cs], tables[5, :, cs])
+            dk = rotated(grad_k[:, :, cs], tables[6, :, cs], tables[7, :, cs])
             low = jnp.concatenate([dq, dk, grad_v[:, :, cs]], axis=0).astype(bfloat)
-            low = low.reshape(3 * width, TILE)
+            low = low.reshape(3 * width, CHUNK)
             grad_proj[:, cs] = low
             grad_normed = dot(qkv_w[l], low)
             u, inv = inputs[l, :, cs], inverse1[l, :, cs]
@@ -412,20 +402,17 @@
             grad_gains[slot, 0] += partial
             grad_u = grad_u + grad[:, cs]
             grad[:, cs] = grad_u.astype(bfloat).astype(single)
-            grad_u = grad_u * jnp.where(l == 0, inverse_spread, 1.0)
-
-            @pl.when(l == section)
-            def _():
-                kept_grad[0, :, cs] = grad_u
-
-            @pl.when(l != section)
-            def _():
-                sent_grad[0, :, cs] = grad_u.astype(bfloat)
-
+            grad_inputs[l, :, cs] = grad_u
         grad_qkv[slot] += dot_nt(normed[l], grad_proj[...])
         return carry
 
     lax.fori_loop(0, 2, backward, 0)
+
+    grad_inputs[0] = grad_inputs[0] * inverse_spread
+    kept_out[0] = inputs[section + 1].astype(bfloat)
+    sent_out[0] = inputs[2 - section].astype(bfloat)
+    kept_grad[0] = grad_inputs[section]
+    sent_grad[0] = grad_inputs[1 - section].astype(bfloat)
 
     @pl.when(step == pl.num_programs(0) - 1)
     def _():
@@ -453,7 +440,11 @@
     frequency = 10000.0 ** (-np.arange(HALF, dtype=np.float64) / HALF)
     frequency = frequency.astype(np.float32)
     angles = np.arange(length, dtype=np.float32)[None, :] * frequency[:, None]
-    return np.cos(angles).astype(np.float32), np.sin(angles).astype(np.float32)
+    cos, sin = np.cos(angles), np.sin(angles)
+    query, grad_query, grad_key = HEAD**-0.5 * LOG2E, HEAD**-0.5, 1.0 / LOG2E
+    tables = [cos, sin, cos * query, sin * query]
+    tables += [cos * grad_query, -sin * grad_query, cos * grad_key, -sin * grad_key]
+    return np.stack(tables).astype(np.float32)
 
 
 def train(section, rows, raw, series_ids, median, scale, cotangent, own, other):
@@ -462,8 +453,8 @@
     heads = width // HEAD
     hidden = own[4].shape[1]
     place = jnp.stack([section, section * count]).astype(jnp.int32)
-    cosine, sine = rotary_tables(length)
-    operands = (raw, cotangent) + own + other + (jnp.asarray(cosine), jnp.asarray(sine))
+    tables = jnp.asarray(rotary_tables(length))
+    operands = (raw, cotangent) + own + other + (tables,)
     smem = pl.BlockSpec(memory_space=pltpu.SMEM)
 
     def whole(array):
@@ -493,7 +484,7 @@
         v((2, width, width), single),
         v((2, width, 2 * hidden), single),
         v((2, width, hidden), single),
-        v((2, width, length), single),
+        v((3, width, length), single),
         v((2, 1, length), single),
         v((2, width, length), bfloat),
         v((2, heads, HEAD, length), bfloat),
@@ -519,6 +510,7 @@
         v((heads, HEAD, length), single),
         v((3 * width, length), bfloat),
         v((2, 2, TILE, TILE), bfloat),
+        v((2, width, length), single),
     ]
     return pl.pallas_call(
         functools.partial(train_kernel, heads, hidden),

time: 209 us -> 189 us (0.904)
  Pallas kernels: 197 us -> 177 us
    pallas_call x1, Pallas kernels: 165 us -> 145 us  [train(): pl.pallas_call(functools.partial(train_kernel, heads, hidden), grid_spec=...]
where the time goes in v3:
time: 189 us
  Pallas kernels  177 us (94%)
  local copies, waits for them, and re-layouts  9.88 us (5%)
    pallas_call x1, Pallas kernels, train(): pl.pallas_call(functools.partial(train_kernel, heads, hidden), grid_spec=...  145 us
    pallas_call x1, Pallas kernels, reduce(): pl.pallas_call(functools.partial(reduce_kernel, sizes), out_shape=(shape(...  30 us
    unnamed x17, local copies, waits for them, and re-layouts  8.78 us

profile of v3, /device:TPU:0, one launch (start us, length us, event | category | flops | bytes accessed | tf_op | source)
XLA Modules:
  0.0 188.7 jit_solution(9452679679302134374)
XLA Ops:
  0.6 0.6 pad_add_fusion.place
  1.2 2.5 %shard_map.162 = (f32[2,144]{1,0:T(2,128)}, bf16[144,432]{1,0:T(8,128)(2,1)}, bf16[144,144]{1,0:T(8,128)(2,1)}, bf16[144,768]{1,0:T(8,128)(2,1)}, bf16[144,384]{1,0:T(8,128)(2,1)}) custom-call(f32[2,144]{1,0:T(2,128)} %bitcast.39, bf16[144,432]{1,0:T(8,128)(2,1)} %bitcast.33, bf16[144,144]{1,0:T(8,128)(2,1)} %bitcast.37, bf16[144,768]{1,0:T(8,128)(2,1)} %bitcast.31, ...), custom_call_target="tpu_custom_call" | custom-call | tf_op jit(solution)/shard_map/pallas_call | solution.py:569
  3.7 144.8 %shard_map.163 = (bf16[8,144,1024]{2,1,0:T(8,128)(2,1)}, f32[8,144,1024]{2,1,0:T(8,128)}, bf16[4,144,1024]{2,1,0:T(8,128)(2,1)}, bf16[4,144,1024]{2,1,0:T(8,128)...) custom-call(s32[2]{0:T(128)} %pad_add_fusion.place, s32[8]{0:T(128)} %series_ids.1, f32[128]{0:T(128)} %median.1, ...), custom_call_target="tpu_custom_call" | custom-call | tf_op jit(solution)/shard_map/pallas_call | solution.py:515
  148.5 0.0 copy-start
  148.5 1.3 copy-done
  149.8 0.0 copy-start.1
  149.8 1.3 copy-done.1
  151.0 0.0 copy-start.2
  151.0 1.2 copy-done.2
  152.3 0.0 copy-start.3
  152.3 1.0 copy-done.3
  153.3 0.0 copy-start.4
  153.3 30.0 %shard_map.164 = (bf16[4,144,1024]{2,1,0:T(8,128)(2,1)S(1)}, bf16[4,144,1024]{2,1,0:T(8,128)(2,1)S(1)}, f32[2,144]{1,0:T(2,128)S(1)}, f32[144,432]{1,0:T(8,128)S...) custom-call(f32[2048,128]{1,0:T(8,128)S(1)} %copy-done.2, ...), custom_call_target="tpu_custom_call" | custom-call | tf_op jit(solution)/shard_map/pallas_call | solution.py:707
  183.3 1.1 constant_dynamic-update-slice_fusion
  184.4 0.0 copy-done.4
  184.4 0.3 convert_dynamic-update-slice_fusion
  184.7 0.0 copy-start.5
  184.7 0.6 copy.25
  185.3 1.3 copy.26
  186.6 0.7 copy.27
  187.2 0.8 copy.28
  188.0 0.7 copy.29
  188.7 0.0 copy-done.5
Async XLA Ops:
  148.5 1.3 copy-start
  149.8 1.3 copy-start.1
  151.0 1.2 copy-start.2
  152.3 1.0 copy-start.3
  153.3 31.1 %copy-start.4 = (f32[8,144,1024]{2,1,0:T(8,128)S(1)}, f32[8,144,1024]{2,1,0:T(8,128)}, u32[]{:S(2)}) copy-start(f32[8,144,1024]{2,1,0:T(8,128)} %get-tuple-element.36) | copy-start | bytes 14155780
  184.7 4.0 %copy-start.5 = (f32[8,144,1024]{2,1,0:T(8,128)}, f32[8,144,1024]{2,1,0:T(8,128)S(1)}, u32[]{:S(2)}) copy-start(f32[8,144,1024]{2,1,0:T(8,128)S(1)} %convert_dynamic-update-slice_fusion) | copy-start | bytes 14155780

commit v4 on v3

--- a/solution.py
+++ b/solution.py
@@ -13,6 +13,7 @@
 HALF = HEAD // 2
 TILE = 256
 CHUNK = 512
+VMEM_LIMIT = 64 * 2**20 - 2**16
 EPSILON = 1e-06
 LOG2E = math.log2(math.e)
 QKV_REST = 48
@@ -528,7 +529,7 @@
             shape((count, width, length), bfloat),
         )
         + totals,
-        compiler_params=pltpu.CompilerParams(vmem_limit_bytes=64 * 2**20 - 2**16),
+        compiler_params=pltpu.CompilerParams(vmem_limit_bytes=VMEM_LIMIT),
     )(place, series_ids, median, scale, *operands)
 
 
@@ -572,7 +573,9 @@
         in_specs=[anywhere] * count,
         out_specs=[anywhere] * count,
         scratch_shapes=[pltpu.SemaphoreType.DMA((count,)), pltpu.SemaphoreType.DMA((count,))],
-        compiler_params=pltpu.CompilerParams(collective_id=0, has_side_effects=True),
+        compiler_params=pltpu.CompilerParams(
+            collective_id=0, has_side_effects=True, vmem_limit_bytes=VMEM_LIMIT
+        ),
     )(*weights)
 
 
@@ -593,19 +596,15 @@
     sent_grad,
     far_out,
     far_grad,
-    grad_gains,
-    grad_qkv,
-    grad_out,
-    grad_gate_up,
-    grad_down,
+    gathered,
     arrived,
     *scratch,
 ):
     count = len(sizes)
     parts = scratch[:count]
     slots = scratch[count : 2 * count]
-    wholes = scratch[2 * count : 3 * count]
-    last, swap_send, swap_recv, sum_send, sum_recv, gather_send, gather_recv = scratch[3 * count :]
+    wholes = (gathered,) + scratch[2 * count : 3 * count - 1]
+    last, swap_send, swap_recv, sum_send, sum_recv, gather_send, gather_recv = scratch[3 * count - 1 :]
     me = lax.axis_index("dp")
     places, groups = [], []
     stride = 1
@@ -633,11 +632,11 @@
         return c
 
     near = copy(other_total, arrived, swap_send.at[0], swap_recv.at[0], partner())
+    near.wait()
     far = [
         copy(sent_out, far_out, swap_send.at[1], swap_recv.at[1], partner()),
         copy(sent_grad, far_grad, swap_send.at[2], swap_recv.at[2], partner()),
     ]
-    near.wait()
     parts[0][...] = (own_total[...] + arrived[...].astype(single)).astype(bfloat)
     first = 0
     starts = []
@@ -676,21 +675,41 @@
         for c in copies:
             c.wait()
         source = wholes[n]
+    for c in far:
+        c.wait()
+
+
+def unpack_kernel(gathered, grad_gains, grad_qkv, grad_out, grad_gate_up, grad_down):
     width = grad_qkv.shape[0]
     block = 0
     for ref in (grad_gate_up, grad_down, grad_qkv, grad_out):
         for n in range(0, ref.shape[1] - 127, 128):
-            ref[:, n : n + 128] = source[block * width : (block + 1) * width, :].astype(single)
+            ref[:, n : n + 128] = gathered[block * width : (block + 1) * width, :].astype(single)
             block += 1
-    rest = source[block * width : (block + 1) * width, :].astype(single)
+    rest = gathered[block * width : (block + 1) * width, :].astype(single)
     grad_qkv[:, 3 * width - QKV_REST :] = rest[:, :QKV_REST]
     grad_out[:, width - OUT_REST :] = rest[:, QKV_REST : QKV_REST + OUT_REST]
     grad_gains[...] = rest.T[QKV_REST + OUT_REST : QKV_REST + OUT_REST + 2, :]
-    for c in far:
-        c.wait()
-
-
-def reduce(devices, own_total, other_total, sent_out, sent_grad, width, hidden):
+
+
+def unpack(gathered, width, hidden):
+    shape = jax.ShapeDtypeStruct
+    vmem = pl.BlockSpec(memory_space=pltpu.VMEM)
+    return pl.pallas_call(
+        unpack_kernel,
+        out_shape=(
+            shape((2, width), single),
+            shape((width, 3 * width), single),
+            shape((width, width), single),
+            shape((width, 2 * hidden), single),
+            shape((width, hidden), single),
+        ),
+        in_specs=[vmem],
+        out_specs=[vmem] * 5,
+    )(gathered)
+
+
+def reduce(devices, own_total, other_total, sent_out, sent_grad):
     sizes = group_sizes(devices)
     rows = own_total.shape[0]
     v = pltpu.VMEM
@@ -709,22 +728,18 @@
         out_shape=(
             shape(sent_out.shape, bfloat),
             shape(sent_grad.shape, bfloat),
-            shape((2, width), single),
-            shape((width, 3 * width), single),
-            shape((width, width), single),
-            shape((width, 2 * hidden), single),
-            shape((width, hidden), single),
+            shape((rows, 128), bfloat),
         ),
         in_specs=[vmem, vmem, anywhere, anywhere],
-        out_specs=[anywhere, anywhere] + [vmem] * 5,
+        out_specs=[anywhere, anywhere, vmem],
         scratch_shapes=[v((rows, 128), bfloat)]
         + parts
         + slots
-        + parts
+        + parts[1:]
         + [v((left, 128), bfloat), dma((3,)), dma((3,))]
         + [dma((links,))] * 4,
         compiler_params=pltpu.CompilerParams(
-            collective_id=1, has_side_effects=True, vmem_limit_bytes=40 * 2**20
+            collective_id=1, has_side_effects=True, vmem_limit_bytes=VMEM_LIMIT
         ),
     )(own_total, other_total, sent_out, sent_grad)
 
@@ -753,9 +768,8 @@
     kept_out, kept_grad, sent_out, sent_grad, own_total, other_total = train(
         section, rows, turned(raw), series_ids, median, scale, turned(cotangent), own, other
     )
-    far_out, far_grad, gain, qkv, out, gate_up, down = reduce(
-        devices, own_total, other_total, sent_out, sent_grad, width, hidden
-    )
+    far_out, far_grad, gathered = reduce(devices, own_total, other_total, sent_out, sent_grad)
+    gain, qkv, out, gate_up, down = unpack(gathered, width, hidden)
     place = ((1 - section) * count, 0, 0)
     layer_outputs = lax.dynamic_update_slice(kept_out, far_out, place)
     input_grads = lax.dynamic_update_slice(kept_grad, far_grad.astype(single), place)

time: 189 us -> 187 us (0.989)
  local copies, waits for them, and re-layouts: 9.88 us -> 2.47 us
  Pallas kernels: 177 us -> 181 us
    unnamed x17 -> x2, local copies, waits for them, and re-layouts: 8.78 us -> 0.01 us
    pallas_call x0 -> x1, Pallas kernels: none -> 2.08 us  [unpack(): pl.pallas_call(unpack_kernel, out_shape=(shape((2, width), single), shape...]
    pallas_call x1, Pallas kernels: 30 us -> 32 us  [reduce(): pl.pallas_call(functools.partial(reduce_kernel, sizes), out_shape=(shape(...]
where the time goes in v4:
time: 187 us
  Pallas kernels  181 us (97%)
  local copies, waits for them, and re-layouts  2.47 us (1%)
  other arithmetic  2.28 us (1%)
    pallas_call x1, Pallas kernels, train(): pl.pallas_call(functools.partial(train_kernel, heads, hidden), grid_spec=...  145 us
    pallas_call x1, Pallas kernels, reduce(): pl.pallas_call(functools.partial(reduce_kernel, sizes), out_shape=(shape(...  32 us

profile of v4, /device:TPU:0, one launch (start us, length us, event | category | flops | bytes accessed | tf_op | source)
XLA Modules:
  0.0 186.7 jit_solution(4844323926169738192)
XLA Ops:
  0.6 0.6 pad_add_fusion.place
  1.2 2.5 %shard_map.162 = (f32[2,144]{1,0:T(2,128)}, bf16[144,432]{1,0:T(8,128)(2,1)}, bf16[144,144]{1,0:T(8,128)(2,1)}, bf16[144,768]{1,0:T(8,128)(2,1)}, bf16[144,384]{1,0:T(8,128)(2,1)}) custom-call(f32[2,144]{1,0:T(2,128)} %bitcast.34, bf16[144,432]{1,0:T(8,128)(2,1)} %bitcast.28, bf16[144,144]{1,0:T(8,128)(2,1)} %bitcast.32, bf16[144,768]{1,0:T(8,128)(2,1)} %bitcast.26, ...), custom_call_target="tpu_custom_call" | custom-call | tf_op jit(solution)/shard_map/pallas_call | solution.py:570
  3.7 144.8 %shard_map.163 = (bf16[8,144,1024]{2,1,0:T(8,128)(2,1)}, f32[8,144,1024]{2,1,0:T(8,128)}, bf16[4,144,1024]{2,1,0:T(8,128)(2,1)}, bf16[4,144,1024]{2,1,0:T(8,128)...) custom-call(s32[2]{0:T(128)} %pad_add_fusion.place, s32[8]{0:T(128)} %series_ids.1, f32[128]{0:T(128)} %median.1, ...), custom_call_target="tpu_custom_call" | custom-call | tf_op jit(solution)/shard_map/pallas_call | solution.py:516
  148.5 32.0 %shard_map.164 = (bf16[4,144,1024]{2,1,0:T(8,128)(2,1)}, bf16[4,144,1024]{2,1,0:T(8,128)(2,1)}, bf16[2048,128]{1,0:T(8,128)(2,1)}) custom-call(f32[2048,128]{1,0:T(8,128)} %get-tuple-element.32.own_total, bf16[2048,128]{1,0:T(8,128)(2,1)} %get-tuple-element.33.other_total, bf16[4,144,1024]{2,1,0:T(8,128)(2,1)} %get-tuple-element.34.sent_out, ...), custom_call_target="tpu_custom_call" | custom-call | tf_op jit(solution)/shard_map/pallas_call | solution.py:726
  180.5 0.0 copy-start
  180.5 2.5 %constant_dynamic-update-slice_fusion = bf16[8,144,1024]{2,1,0:T(8,128)(2,1)} fusion(bf16[8,144,1024]{2,1,0:T(8,128)(2,1)} %get-tuple-element.31, bf16[4,144,1024]{2,1,0:T(8,128)(2,1)} %get-tuple-element.36, s32[]{:T(128)S(6)} %select_n.4), kind=kLoop, calls=%fused_computation.2 | loop fusion | bytes 2359300 | tf_op jit(solution)/shard_map/dynamic_update_slice | solution.py:774
  183.0 0.0 copy-done
  183.0 1.7 convert_dynamic-update-slice_fusion
  184.7 2.1 %shard_map.165 = (f32[2,144]{1,0:T(2,128)}, f32[144,432]{1,0:T(8,128)}, f32[144,144]{1,0:T(8,128)}, f32[144,768]{1,0:T(8,128)}, f32[144,384]{1,0:T(8,128)}) custom-call(bf16[2048,128]{1,0:T(8,128)(2,1)} %get-tuple-element.39.gathered), custom_call_target="tpu_custom_call" | custom-call | tf_op jit(solution)/shard_map/pallas_call | solution.py:698
Async XLA Ops:
  180.5 2.5 %copy-start = (bf16[4,144,1024]{2,1,0:T(8,128)(2,1)S(1)}, bf16[4,144,1024]{2,1,0:T(8,128)(2,1)}, u32[]{:S(2)}) copy-start(bf16[4,144,1024]{2,1,0:T(8,128)(2,1)} %get-tuple-element.38) | copy-start | bytes 3538948

commit v5 on v4

--- a/solution.py
+++ b/solution.py
@@ -13,9 +13,12 @@
 HALF = HEAD // 2
 TILE = 256
 CHUNK = 512
+ROWS = 128
+TURN_AT = 3
+BACK_AT = 6
 VMEM_LIMIT = 64 * 2**20 - 2**16
 EPSILON = 1e-06
-LOG2E = math.log2(math.e)
+EXPONENT = HEAD**-0.5 * math.log2(math.e)
 QKV_REST = 48
 OUT_REST = 16
 MESH = pl.DeviceIdType.MESH
@@ -128,7 +131,6 @@
     grad_att,
     grad_q,
     grad_k,
-    grad_v,
     grad_proj,
     flipped,
     grad_inputs,
@@ -142,6 +144,7 @@
     width, length = inputs.shape[1:]
     tiles = length // TILE
     chunks = [slice(n, n + CHUNK) for n in range(0, length, CHUNK)]
+    columns = [slice(n, n + TILE) for n in range(0, length, TILE)]
 
     @pl.when(step == 0)
     def _():
@@ -161,13 +164,15 @@
             qkv_t[l] = turned(qkv[...])
             out_w[l] = out[...]
             out_t[l] = turned(out[...])
-            gate_up_w[l] = both[...]
-            gate_up_t[l] = turned(both[...])
+            column = lax.broadcasted_iota(jnp.int32, both.shape, 1)
+            halved = both[...].astype(single) * jnp.where(column < hidden, 0.5, 1.0)
+            gate_up_w[l] = halved.astype(bfloat)
+            gate_up_t[l] = halved.T.astype(bfloat)
             down_t[l] = down[...]
             down_w[l] = turned(down[...])
 
-    def gain_of(l, part):
-        return jnp.concatenate([gains[l, part]] * (CHUNK // 128), axis=1)
+    def gain_of(l, part, count=CHUNK):
+        return jnp.concatenate([gains[l, part]] * (count // 128), axis=1)
 
     inputs[0] = (raw[0].astype(single) - centre) * inverse_spread
     grad[...] = cotangent[0].astype(single)
@@ -192,13 +197,10 @@
             low = (u * inv * gain_of(l, 0)).astype(bfloat)
             normed[l, :, cs] = low
             projected = dot(qkv_t[l], low).reshape(3 * heads, HEAD, CHUNK)
-            q = rotated(projected[:heads], tables[2, :, cs], tables[3, :, cs])
-            k = rotated(projected[heads : 2 * heads], tables[0, :, cs], tables[1, :, cs])
-            queries[l, :, :, cs] = q.astype(bfloat)
-            keys[l, :, :, cs] = k.astype(bfloat)
+            q, k = projected[:heads], projected[heads : 2 * heads]
+            grad_q[:, :, cs] = q
+            grad_k[:, :, cs] = k
             values[l, :, :HEAD, cs] = projected[2 * heads :].astype(bfloat)
-            for h in range(heads):
-                rows_major[h, cs, :HEAD] = k[h].T.astype(bfloat)
             squares = lambda v: dot(of_head, (v * v).astype(bfloat).reshape(width, CHUNK))
             largest_q = jnp.maximum(largest_q, squares(q))
             largest_k = jnp.maximum(largest_k, squares(k))
@@ -214,14 +216,24 @@
             attended32[l, h, :, js] = out
             attended[l, h, :, js] = out.astype(bfloat)
 
-        small = bound <= 1e4
+        def turn(three):
+            hs = slice(three * 3, three * 3 + 3)
+            for cs in chunks:
+                q = rotated(grad_q[hs, :, cs], tables[0, :, cs], tables[1, :, cs])
+                k = rotated(grad_k[hs, :, cs], tables[0, :, cs], tables[1, :, cs])
+                queries[l, hs, :, cs] = q.astype(bfloat)
+                keys[l, hs, :, cs] = k.astype(bfloat)
+                for g in range(3):
+                    rows_major[three * 3 + g, cs, :HEAD] = k[g].T.astype(bfloat)
+
+        small = bound * EXPONENT**2 <= 1e4
 
         @pl.when(small)
         def _():
             pairs = lanes(tiles)
             ahead = 3
 
-            def some(three, carry):
+            def some(three):
                 scores = {}
 
                 def score(m):
@@ -235,11 +247,13 @@
                     score(m)
                 totals = {}
                 for m, pair in enumerate(pairs):
+                    if m == TURN_AT and (three + 1) * 3 < heads:
+                        turn(three + 1)
                     if m + ahead < len(pairs):
                         score(m + ahead)
                     ready = []
                     for side, (g, j, k) in enumerate(pair):
-                        e = jnp.exp2(scores.pop((m, side)))
+                        e = jnp.exp2(scores.pop((m, side)) * EXPONENT)
                         if k == j:
                             e = jnp.where(causal(e), e, 0.0)
                         e = e.astype(bfloat)
@@ -252,17 +266,21 @@
                         totals[g, j] = totals[g, j] + part if k else part
                         if k == j:
                             finish(h, j, totals.pop((g, j)))
-                return carry
-
-            lax.fori_loop(0, heads // 3, some, 0)
+
+            turn(0)
+            for three in range(heads // 3):
+                some(three)
 
         @pl.when(jnp.logical_not(small))
         def _():
+            for three in range(heads // 3):
+                turn(three)
+
             def one(h, carry):
                 for j in range(tiles):
                     count = (j + 1) * TILE
                     js = slice(j * TILE, (j + 1) * TILE)
-                    score = dot(rows_major[h, :count, :HEAD], queries[l, h, :, js])
+                    score = dot(rows_major[h, :count, :HEAD], queries[l, h, :, js]) * EXPONENT
                     rows = lax.broadcasted_iota(jnp.int32, score.shape, 0)
                     columns = lax.broadcasted_iota(jnp.int32, score.shape, 1) + j * TILE
                     score = jnp.where(rows <= columns, score, -1e30)
@@ -280,17 +298,20 @@
             residual[l, :, cs] = res
             inv = rms_scale(res)
             inverse2[l, :, cs] = inv
-            low = (res * inv * gain_of(l, 1)).astype(bfloat)
-            mid[l, :, cs] = low
-            both = dot(gate_up_t[l], low)
-            gate, up = both[:hidden], both[hidden:]
-            sig = 0.5 * jnp.tanh(0.5 * gate) + 0.5
-            swish = gate * sig
-            gate_up[l, :hidden, cs] = up * (sig + swish * (1.0 - sig))
-            gate_up[l, hidden:, cs] = swish
-            act = (swish * up).astype(bfloat)
-            activated[l, :, cs] = act
-            result = res + dot(down_t[l], act)
+            mid[l, :, cs] = (res * inv * gain_of(l, 1)).astype(bfloat)
+        for cs in columns:
+            low = mid[l, :, cs]
+            for n in range(0, hidden, ROWS):
+                half = dot(gate_up_t[l, n : n + ROWS], low)
+                up = dot(gate_up_t[l, hidden + n : hidden + n + ROWS], low)
+                t = jnp.tanh(half)
+                twice = 1.0 + t
+                swish = half * twice
+                gate_up[l, n : n + ROWS, cs] = up * (twice + swish * (1.0 - t))
+                gate_up[l, hidden + n : hidden + n + ROWS, cs] = swish
+                activated[l, n : n + ROWS, cs] = (swish * up).astype(bfloat)
+        for cs in chunks:
+            result = residual[l, :, cs] + dot(down_t[l], activated[l, :, cs])
             inputs[l + 1, :, cs] = result.astype(bfloat).astype(single)
         return carry
 
@@ -299,16 +320,17 @@
     def backward(turn, carry):
         l = 1 - turn
         slot = lax.rem(l + section, 2)
+        for cs in columns:
+            low = grad[:, cs].astype(bfloat)
+            grad_low[:, cs] = low
+            for n in range(0, hidden, ROWS):
+                grad_act = dot(down_w[l, n : n + ROWS], low)
+                for m in (n, hidden + n):
+                    factor = gate_up[l, m : m + ROWS, cs]
+                    grad_pre[m : m + ROWS, cs] = (grad_act * factor).astype(bfloat)
         for cs in chunks:
             g = grad[:, cs]
-            low = g.astype(bfloat)
-            grad_low[:, cs] = low
-            grad_act = dot(down_w[l], low)
-            pre = jnp.concatenate(
-                [grad_act * gate_up[l, :hidden, cs], grad_act * gate_up[l, hidden:, cs]], axis=0
-            ).astype(bfloat)
-            grad_pre[:, cs] = pre
-            grad_mid = dot(gate_up_w[l], pre)
+            grad_mid = dot(gate_up_w[l], grad_pre[:, cs])
             res, inv = residual[l, :, cs], inverse2[l, :, cs]
             grad_res, partial = rms_backward(grad_mid, res, inv, gain_of(l, 1))
             grad_gains[slot, 1] += partial
@@ -328,14 +350,23 @@
         grad_gate_up[slot] += dot_nt(mid[l], grad_pre[...])
         grad_out[slot] += dot_nt(attended[l].reshape(width, length), grad_res_low[...])
 
-        for h in range(heads):
-            rows_major[h] = grad_att[h].astype(single).T.astype(bfloat)
+        def turn(three):
+            for h in range(three * 3, three * 3 + 3):
+                rows_major[h] = grad_att[h].T
+
+        def turn_back(three):
+            hs = slice(three * 3, three * 3 + 3)
+            for cs in chunks:
+                dq = rotated(grad_q[hs, :, cs], tables[2, :, cs], tables[3, :, cs])
+                dk = rotated(grad_k[hs, :, cs], tables[2, :, cs], tables[3, :, cs])
+                grad_proj[hs, :, cs] = dq.astype(bfloat)
+                grad_proj[three * 3 + heads : three * 3 + heads + 3, :, cs] = dk.astype(bfloat)
 
         pairs = lanes(tiles)
         ahead = 2
         half = TILE // 2
 
-        def some(three, carry):
+        def some(three):
             products, held, sums = {}, {}, {}
 
             def product(m, part):
@@ -355,6 +386,10 @@
                 product(m, 0)
                 product(m, 1)
             for m in range(len(pairs) + 1):
+                if m == TURN_AT and (three + 1) * 3 < heads:
+                    turn(three + 1)
+                if m == BACK_AT and three > 0:
+                    turn_back(three - 1)
                 now = pairs[m] if m < len(pairs) else ()
                 before = pairs[m - 1] if m > 0 else ()
                 product(m + ahead, 0)
@@ -383,20 +418,21 @@
                     turned = flipped[(m - 1) % 2, side]
                     add("q", j, side, g, dot(keys[l, three * 3 + g, :, ks], turned))
             for g in range(3):
-                for name, ref in (("q", grad_q), ("k", grad_k), ("v", grad_v)):
+                h = three * 3 + g
+                for name, ref in (("q", grad_q), ("k", grad_k), ("v", grad_proj)):
                     for t in range(tiles):
                         found = [sums[name, g, t, n] for n in range(2) if (name, g, t, n) in sums]
-                        ref[three * 3 + g, :, t * TILE : (t + 1) * TILE] = sum(found[1:], found[0])
-            return carry
-
-        lax.fori_loop(0, heads // 3, some, 0)
+                        place = h + 2 * heads if name == "v" else h
+                        total = sum(found[1:], found[0]).astype(ref.dtype)
+                        ref[place, :, t * TILE : (t + 1) * TILE] = total
+
+        turn(0)
+        for three in range(heads // 3):
+            some(three)
+        turn_back(heads // 3 - 1)
 
         for cs in chunks:
-            dq = rotated(grad_q[:, :, cs], tables[4, :, cs], tables[5, :, cs])
-            dk = rotated(grad_k[:, :, cs], tables[6, :, cs], tables[7, :, cs])
-            low = jnp.concatenate([dq, dk, grad_v[:, :, cs]], axis=0).astype(bfloat)
-            low = low.reshape(3 * width, CHUNK)
-            grad_proj[:, cs] = low
+            low = grad_proj[:, :, cs].reshape(3 * width, CHUNK)
             grad_normed = dot(qkv_w[l], low)
             u, inv = inputs[l, :, cs], inverse1[l, :, cs]
             grad_u, partial = rms_backward(grad_normed, u, inv, gain_of(l, 0))
@@ -404,7 +440,7 @@
             grad_u = grad_u + grad[:, cs]
             grad[:, cs] = grad_u.astype(bfloat).astype(single)
             grad_inputs[l, :, cs] = grad_u
-        grad_qkv[slot] += dot_nt(normed[l], grad_proj[...])
+        grad_qkv[slot] += dot_nt(normed[l], grad_proj[...].reshape(3 * width, length))
         return carry
 
     lax.fori_loop(0, 2, backward, 0)
@@ -420,7 +456,9 @@
         for slot, total in ((0, own_total), (1, other_total)):
             blocks = []
             for ref in (grad_gate_up, grad_down, grad_qkv, grad_out):
-                blocks += [ref[slot, :, n : n + 128] for n in range(0, ref.shape[2] - 127, 128)]
+                for n in range(0, ref.shape[2] - 127, 128):
+                    doubled = ref is grad_gate_up and n < hidden
+                    blocks.append(ref[slot, :, n : n + 128] * (0.5 if doubled else 1.0))
             lane = lax.broadcasted_iota(jnp.int32, (width, 128), 1)
             spare = grad_qkv[slot, :, 3 * width - QKV_REST :]
             out_rest = grad_out[slot, :, width - OUT_REST :]
@@ -442,9 +480,7 @@
     frequency = frequency.astype(np.float32)
     angles = np.arange(length, dtype=np.float32)[None, :] * frequency[:, None]
     cos, sin = np.cos(angles), np.sin(angles)
-    query, grad_query, grad_key = HEAD**-0.5 * LOG2E, HEAD**-0.5, 1.0 / LOG2E
-    tables = [cos, sin, cos * query, sin * query]
-    tables += [cos * grad_query, -sin * grad_query, cos * grad_key, -sin * grad_key]
+    tables = [cos, sin, cos * HEAD**-0.5, -sin * HEAD**-0.5]
     return np.stack(tables).astype(np.float32)
 
 
@@ -508,8 +544,7 @@
         v((heads, 2 * HEAD, length), bfloat),
         v((heads, HEAD, length), single),
         v((heads, HEAD, length), single),
-        v((heads, HEAD, length), single),
-        v((3 * width, length), bfloat),
+        v((3 * heads, HEAD, length), bfloat),
         v((2, 2, TILE, TILE), bfloat),
         v((2, width, length), single),
     ]
@@ -679,34 +714,70 @@
         c.wait()
 
 
-def unpack_kernel(gathered, grad_gains, grad_qkv, grad_out, grad_gate_up, grad_down):
-    width = grad_qkv.shape[0]
-    block = 0
-    for ref in (grad_gate_up, grad_down, grad_qkv, grad_out):
-        for n in range(0, ref.shape[1] - 127, 128):
-            ref[:, n : n + 128] = gathered[block * width : (block + 1) * width, :].astype(single)
-            block += 1
-    rest = gathered[block * width : (block + 1) * width, :].astype(single)
-    grad_qkv[:, 3 * width - QKV_REST :] = rest[:, :QKV_REST]
-    grad_out[:, width - OUT_REST :] = rest[:, QKV_REST : QKV_REST + OUT_REST]
-    grad_gains[...] = rest.T[QKV_REST + OUT_REST : QKV_REST + OUT_REST + 2, :]
-
-
-def unpack(gathered, width, hidden):
+def finish_kernel(
+    place,
+    gathered,
+    far_out,
+    far_grad,
+    kept_out,
+    kept_grad,
+    layer_outputs,
+    input_grads,
+    grad_gains,
+    grad_qkv,
+    grad_out,
+    grad_gate_up,
+    grad_down,
+):
+    layer_outputs[...] = far_out[...]
+    input_grads[...] = far_grad[...].astype(single)
+
+    @pl.when(pl.program_id(0) == 0)
+    def _():
+        width = grad_qkv.shape[0]
+        block = 0
+        for ref in (grad_gate_up, grad_down, grad_qkv, grad_out):
+            for n in range(0, ref.shape[1] - 127, 128):
+                rows = slice(block * width, (block + 1) * width)
+                ref[:, n : n + 128] = gathered[rows, :].astype(single)
+                block += 1
+        rest = gathered[block * width : (block + 1) * width, :].astype(single)
+        grad_qkv[:, 3 * width - QKV_REST :] = rest[:, :QKV_REST]
+        grad_out[:, width - OUT_REST :] = rest[:, QKV_REST : QKV_REST + OUT_REST]
+        grad_gains[...] = rest.T[QKV_REST + OUT_REST : QKV_REST + OUT_REST + 2, :]
+
+
+def finish(place, gathered, far_out, far_grad, kept_out, kept_grad, hidden):
     shape = jax.ShapeDtypeStruct
-    vmem = pl.BlockSpec(memory_space=pltpu.VMEM)
+    count, width, length = far_out.shape
+    anywhere = pl.BlockSpec(memory_space=pl.ANY)
+    block = pl.BlockSpec((1, width, length), lambda i, place: (i, 0, 0))
+    placed = pl.BlockSpec((1, width, length), lambda i, place: (place[0] + i, 0, 0))
+    grads = (
+        shape((2, width), single),
+        shape((width, 3 * width), single),
+        shape((width, width), single),
+        shape((width, 2 * hidden), single),
+        shape((width, hidden), single),
+    )
+
+    def whole(array):
+        return pl.BlockSpec(
+            array.shape, lambda i, place: (0, 0), pipeline_mode=pl.Buffered(buffer_count=1)
+        )
+
     return pl.pallas_call(
-        unpack_kernel,
-        out_shape=(
-            shape((2, width), single),
-            shape((width, 3 * width), single),
-            shape((width, width), single),
-            shape((width, 2 * hidden), single),
-            shape((width, hidden), single),
+        finish_kernel,
+        grid_spec=pltpu.PrefetchScalarGridSpec(
+            num_scalar_prefetch=1,
+            grid=(count,),
+            in_specs=[whole(gathered), block, block, anywhere, anywhere],
+            out_specs=[placed, placed] + [whole(g) for g in grads],
         ),
-        in_specs=[vmem],
-        out_specs=[vmem] * 5,
-    )(gathered)
+        out_shape=(shape(kept_out.shape, bfloat), shape(kept_grad.shape, single)) + grads,
+        input_output_aliases={4: 0, 5: 1},
+        compiler_params=pltpu.CompilerParams(vmem_limit_bytes=VMEM_LIMIT),
+    )(place, gathered, far_out, far_grad, kept_out, kept_grad)
 
 
 def reduce(devices, own_total, other_total, sent_out, sent_grad):
@@ -769,10 +840,10 @@
         section, rows, turned(raw), series_ids, median, scale, turned(cotangent), own, other
     )
     far_out, far_grad, gathered = reduce(devices, own_total, other_total, sent_out, sent_grad)
-    gain, qkv, out, gate_up, down = unpack(gathered, width, hidden)
-    place = ((1 - section) * count, 0, 0)
-    layer_outputs = lax.dynamic_update_slice(kept_out, far_out, place)
-    input_grads = lax.dynamic_update_slice(kept_grad, far_grad.astype(single), place)
+    place = jnp.reshape((1 - section) * count, (1,)).astype(jnp.int32)
+    layer_outputs, input_grads, gain, qkv, out, gate_up, down = finish(
+        place, gathered, far_out, far_grad, kept_out, kept_grad, hidden
+    )
     return (
         turned(layer_outputs)[None],
         turned(input_grads)[None],

time: 187 us -> 176 us (0.941)
  Pallas kernels: 181 us -> 174 us
  local copies, waits for them, and re-layouts: 2.47 us -> 0 us
    pallas_call x1, Pallas kernels: 145 us -> 135 us  [train(): pl.pallas_call(functools.partial(train_kernel, heads, hidden), grid_spec=...]
    pallas_call x1, Pallas kernels: 2.08 us -> 4.78 us  [finish(): pl.pallas_call(finish_kernel, grid_spec=pltpu.PrefetchScalarGridSpec(num_...]
    dynamic_update_slice x1 -> x0, local copies, waits for them, and re-layouts: 2.46 us -> none  [on_device(): layer_outputs = lax.dynamic_update_slice(kept_out, far_out, place)]
where the time goes in v5:
time: 176 us; the launch traced here: 175 us
  Pallas kernels  174 us (99%)
    pallas_call x1, Pallas kernels, train(): pl.pallas_call(functools.partial(train_kernel, heads, hidden), grid_spec=...  135 us
    pallas_call x1, Pallas kernels, reduce(): pl.pallas_call(functools.partial(reduce_kernel, sizes), out_shape=(shape(...  32 us
    pallas_call x1, Pallas kernels, finish(): pl.pallas_call(finish_kernel, grid_spec=pltpu.PrefetchScalarGridSpec(num_...  4.78 us

profile of v5, /device:TPU:0, one launch (start us, length us, event | category | flops | bytes accessed | tf_op | source)
XLA Modules:
  0.0 175.4 jit_solution(349893461023527620)
XLA Ops:
  0.6 0.6 pad_add_fusion.place
  1.2 2.5 %shard_map.162 = (f32[2,144]{1,0:T(2,128)}, bf16[144,432]{1,0:T(8,128)(2,1)}, bf16[144,144]{1,0:T(8,128)(2,1)}, bf16[144,768]{1,0:T(8,128)(2,1)}, bf16[144,384]{1,0:T(8,128)(2,1)}) custom-call(f32[2,144]{1,0:T(2,128)} %bitcast.37, bf16[144,432]{1,0:T(8,128)(2,1)} %bitcast.31, bf16[144,144]{1,0:T(8,128)(2,1)} %bitcast.35, bf16[144,768]{1,0:T(8,128)(2,1)} %bitcast.29, ...), custom_call_target="tpu_custom_call" | custom-call | tf_op jit(solution)/shard_map/pallas_call | solution.py:605
  3.7 134.9 %shard_map.163 = (bf16[8,144,1024]{2,1,0:T(8,128)(2,1)}, f32[8,144,1024]{2,1,0:T(8,128)}, bf16[4,144,1024]{2,1,0:T(8,128)(2,1)}, bf16[4,144,1024]{2,1,0:T(8,128)...) custom-call(s32[2]{0:T(128)} %pad_add_fusion.place, s32[8]{0:T(128)} %series_ids.1, f32[128]{0:T(128)} %median.1, ...), custom_call_target="tpu_custom_call" | custom-call | tf_op jit(solution)/shard_map/pallas_call | solution.py:551
  138.6 32.0 %shard_map.164 = (bf16[4,144,1024]{2,1,0:T(8,128)(2,1)}, bf16[4,144,1024]{2,1,0:T(8,128)(2,1)}, bf16[2048,128]{1,0:T(8,128)(2,1)}) custom-call(f32[2048,128]{1,0:T(8,128)} %get-tuple-element.33.own_total, bf16[2048,128]{1,0:T(8,128)(2,1)} %get-tuple-element.34.other_total, bf16[4,144,1024]{2,1,0:T(8,128)(2,1)} %get-tuple-element.35.sent_out, ...), custom_call_target="tpu_custom_call" | custom-call | tf_op jit(solution)/shard_map/pallas_call | solution.py:797
  170.6 4.8 %shard_map.165 = (bf16[8,144,1024]{2,1,0:T(8,128)(2,1)}, f32[8,144,1024]{2,1,0:T(8,128)}, f32[2,144]{1,0:T(2,128)}, f32[144,432]{1,0:T(8,128)}, f32[144,144]{1,0...) custom-call(s32[1]{0:T(128)} %bitcast.place, ...), custom_call_target="tpu_custom_call", output_to_operand_aliasing={{0}: (4, {}), {1}: (5, {})} | custom-call | tf_op jit(solution)/shard_map/pallas_call | solution.py:769

commit v6 on v5

--- a/solution.py
+++ b/solution.py
@@ -14,8 +14,8 @@
 TILE = 256
 CHUNK = 512
 ROWS = 128
-TURN_AT = 3
-BACK_AT = 6
+TURN_AT = 6
+BACK_AT = 8
 VMEM_LIMIT = 64 * 2**20 - 2**16
 EPSILON = 1e-06
 EXPONENT = HEAD**-0.5 * math.log2(math.e)
@@ -59,19 +59,23 @@
     return j * (j + 1) // 2 * TILE
 
 
-def lanes(tiles):
-    full = [(j, k) for j in range(tiles) for k in range(j + 1)]
-    sides = [[(side, j, k) for j, k in full] for side in range(2)]
-    for j in reversed(range(tiles)):
-        side = min(sides, key=len)
-        side += [(2, j, k) for k in range(j + 1)]
-    return list(zip(*sides))
+def lanes(tiles, heads):
+    pairs = []
+    for first in range(0, heads, 3):
+        full = [(j, k) for j in range(tiles) for k in range(j + 1)]
+        sides = [[(first + side, j, k) for j, k in full] for side in range(2)]
+        for j in reversed(range(tiles)):
+            side = min(sides, key=len)
+            side += [(first + 2, j, k) for k in range(j + 1)]
+        pairs += zip(*sides)
+    return pairs
 
 
 def train_kernel(
     heads,
     hidden,
-    place,
+    here,
+    start,
     series_ids,
     median,
     scale,
@@ -136,8 +140,8 @@
     grad_inputs,
 ):
     step = pl.program_id(0)
-    section = place[0]
-    series = place[1] + step
+    section = here[0]
+    series = start[0] + step
     number = series_ids[series]
     centre = median[number]
     inverse_spread = 1.0 / scale[number]
@@ -208,10 +212,10 @@
             jnp.max(largest_q, axis=1, keepdims=True) * jnp.max(largest_k, axis=1, keepdims=True)
         )
 
-        def finish(h, j, total):
+        def finish(h, j, product, total):
             js = slice(j * TILE, (j + 1) * TILE)
-            inverse = 1.0 / total[HEAD : HEAD + 1]
-            out = total[:HEAD] * inverse
+            inverse = 1.0 / total
+            out = product * inverse
             reciprocal[l, h, :, js] = inverse
             attended32[l, h, :, js] = out
             attended[l, h, :, js] = out.astype(bfloat)
@@ -230,46 +234,43 @@
 
         @pl.when(small)
         def _():
-            pairs = lanes(tiles)
-            ahead = 3
-
-            def some(three):
-                scores = {}
-
-                def score(m):
-                    for side, (g, j, k) in enumerate(pairs[m]):
-                        scores[m, side] = dot(
-                            rows_major[three * 3 + g, k * TILE : (k + 1) * TILE, :HEAD],
-                            queries[l, three * 3 + g, :, j * TILE : (j + 1) * TILE],
-                        )
-
-                for m in range(ahead):
-                    score(m)
-                totals = {}
-                for m, pair in enumerate(pairs):
-                    if m == TURN_AT and (three + 1) * 3 < heads:
-                        turn(three + 1)
-                    if m + ahead < len(pairs):
-                        score(m + ahead)
-                    ready = []
-                    for side, (g, j, k) in enumerate(pair):
-                        e = jnp.exp2(scores.pop((m, side)) * EXPONENT)
-                        if k == j:
-                            e = jnp.where(causal(e), e, 0.0)
-                        e = e.astype(bfloat)
-                        first = tile_start(j) + k * TILE
-                        exponents[l, three * 3 + g, first : first + TILE, :] = e.T
-                        ready.append(e)
-                    for side, (g, j, k) in enumerate(pair):
-                        h = three * 3 + g
-                        part = dot(values[l, h, :, k * TILE : (k + 1) * TILE], ready[side])
-                        totals[g, j] = totals[g, j] + part if k else part
-                        if k == j:
-                            finish(h, j, totals.pop((g, j)))
+            pairs = lanes(tiles, heads)
+            group = len(pairs) * 3 // heads
+            ahead = 2
+            scores, products, totals = {}, {}, {}
+
+            def score(m):
+                for side, (h, j, k) in enumerate(pairs[m]):
+                    scores[m, side] = dot(
+                        rows_major[h, k * TILE : (k + 1) * TILE, :HEAD],
+                        queries[l, h, :, j * TILE : (j + 1) * TILE],
+                    )
 
             turn(0)
-            for three in range(heads // 3):
-                some(three)
+            for m in range(ahead):
+                score(m)
+            for m, pair in enumerate(pairs):
+                if m % group == TURN_AT and m + group < len(pairs):
+                    turn(m // group + 1)
+                if m + ahead < len(pairs):
+                    score(m + ahead)
+                ready = []
+                for side, (h, j, k) in enumerate(pair):
+                    e = jnp.exp2(scores.pop((m, side)) * EXPONENT)
+                    if k == j:
+                        e = jnp.where(causal(e), e, 0.0)
+                    part = jnp.sum(e.reshape(TILE // 8, 8, TILE), axis=0)
+                    totals[h, j] = totals[h, j] + part if k else part
+                    e = e.astype(bfloat)
+                    first = tile_start(j) + k * TILE
+                    exponents[l, h, first : first + TILE, :] = e.T
+                    ready.append(e)
+                for side, (h, j, k) in enumerate(pair):
+                    part = dot(values[l, h, :HEAD, k * TILE : (k + 1) * TILE], ready[side])
+                    products[h, j] = products[h, j] + part if k else part
+                    if k == j:
+                        total = jnp.sum(totals.pop((h, j)), axis=0, keepdims=True)
+                        finish(h, j, products.pop((h, j)), total)
 
         @pl.when(jnp.logical_not(small))
         def _():
@@ -284,11 +285,13 @@
                     rows = lax.broadcasted_iota(jnp.int32, score.shape, 0)
                     columns = lax.broadcasted_iota(jnp.int32, score.shape, 1) + j * TILE
                     score = jnp.where(rows <= columns, score, -1e30)
-                    e = jnp.exp2(score - jnp.max(score, axis=0, keepdims=True)).astype(bfloat)
+                    e = jnp.exp2(score - jnp.max(score, axis=0, keepdims=True))
+                    total = jnp.sum(e, axis=0, keepdims=True)
+                    e = e.astype(bfloat)
                     for k in range(j + 1):
                         first = tile_start(j) + k * TILE
                         exponents[l, h, first : first + TILE, :] = e[k * TILE : (k + 1) * TILE].T
-                    finish(h, j, dot(values[l, h, :, :count], e))
+                    finish(h, j, dot(values[l, h, :HEAD, :count], e), total)
                 return carry
 
             lax.fori_loop(0, heads, one, 0)
@@ -328,9 +331,12 @@
                 for m in (n, hidden + n):
                     factor = gate_up[l, m : m + ROWS, cs]
                     grad_pre[m : m + ROWS, cs] = (grad_act * factor).astype(bfloat)
-        for cs in chunks:
+        grad_mids = [dot(gate_up_w[l], grad_pre[:, cs]) for cs in chunks]
+        for n, cs in enumerate(chunks):
+            half = slice(n * 2 * hidden // len(chunks), (n + 1) * 2 * hidden // len(chunks))
+            grad_gate_up[slot, :, half] += dot_nt(mid[l], grad_pre[half, :])
             g = grad[:, cs]
-            grad_mid = dot(gate_up_w[l], grad_pre[:, cs])
+            grad_mid = grad_mids[n]
             res, inv = residual[l, :, cs], inverse2[l, :, cs]
             grad_res, partial = rms_backward(grad_mid, res, inv, gain_of(l, 1))
             grad_gains[slot, 1] += partial
@@ -347,7 +353,6 @@
             rest = jnp.zeros((heads, HALF, CHUNK), single)
             grad_att[:, :, cs] = jnp.concatenate([back * inverse, extra, rest], axis=1).astype(bfloat)
         grad_down[slot] += dot_nt(grad_low[...], activated[l])
-        grad_gate_up[slot] += dot_nt(mid[l], grad_pre[...])
         grad_out[slot] += dot_nt(attended[l].reshape(width, length), grad_res_low[...])
 
         def turn(three):
@@ -362,85 +367,81 @@
                 grad_proj[hs, :, cs] = dq.astype(bfloat)
                 grad_proj[three * 3 + heads : three * 3 + heads + 3, :, cs] = dk.astype(bfloat)
 
-        pairs = lanes(tiles)
+        pairs = lanes(tiles, heads)
+        group = len(pairs) * 3 // heads
         ahead = 2
         half = TILE // 2
-
-        def some(three):
-            products, held, sums = {}, {}, {}
-
-            def product(m, part):
-                if m < len(pairs):
-                    for side, (g, j, k) in enumerate(pairs[m]):
-                        first = j * TILE + part * half
-                        products[m, side, part] = dot(
-                            rows_major[three * 3 + g, first : first + half, :],
-                            values[l, three * 3 + g, :, k * TILE : (k + 1) * TILE],
-                        )
-
-            def add(name, index, side, g, value):
-                key = name, g, index, side
-                sums[key] = sums[key] + value if key in sums else value
-
-            for m in range(ahead):
-                product(m, 0)
-                product(m, 1)
-            for m in range(len(pairs) + 1):
-                if m == TURN_AT and (three + 1) * 3 < heads:
-                    turn(three + 1)
-                if m == BACK_AT and three > 0:
-                    turn_back(three - 1)
-                now = pairs[m] if m < len(pairs) else ()
-                before = pairs[m - 1] if m > 0 else ()
-                product(m + ahead, 0)
-                exps = []
-                for side, (g, j, k) in enumerate(now):
-                    first = tile_start(j) + k * TILE
-                    e = exponents[l, three * 3 + g, first : first + TILE, :]
-                    parts = [
-                        e[p * half : (p + 1) * half] * products.pop((m, side, p)).astype(bfloat)
-                        for p in range(2)
-                    ]
-                    grad_score = jnp.concatenate(parts, axis=0)
-                    flipped[m % 2, side] = grad_score.T
-                    held[m, side] = grad_score
-                    exps.append(e)
-                for side, (g, j, k) in enumerate(now):
-                    js = slice(j * TILE, (j + 1) * TILE)
-                    add("v", k, side, g, dot(grad_att[three * 3 + g, :HEAD, js], exps[side]))
-                product(m + ahead, 1)
-                for side, (g, j, k) in enumerate(before):
-                    js = slice(j * TILE, (j + 1) * TILE)
-                    grad_score = held.pop((m - 1, side))
-                    add("k", k, side, g, dot(queries[l, three * 3 + g, :, js], grad_score))
-                for side, (g, j, k) in enumerate(before):
-                    ks = slice(k * TILE, (k + 1) * TILE)
-                    turned = flipped[(m - 1) % 2, side]
-                    add("q", j, side, g, dot(keys[l, three * 3 + g, :, ks], turned))
-            for g in range(3):
-                h = three * 3 + g
-                for name, ref in (("q", grad_q), ("k", grad_k), ("v", grad_proj)):
-                    for t in range(tiles):
-                        found = [sums[name, g, t, n] for n in range(2) if (name, g, t, n) in sums]
-                        place = h + 2 * heads if name == "v" else h
-                        total = sum(found[1:], found[0]).astype(ref.dtype)
-                        ref[place, :, t * TILE : (t + 1) * TILE] = total
+        products, held, sums = {}, {}, {}
+
+        def product(m, part):
+            if m < len(pairs):
+                for side, (h, j, k) in enumerate(pairs[m]):
+                    first = j * TILE + part * half
+                    products[m, side, part] = dot(
+                        rows_major[h, first : first + half, :],
+                        values[l, h, :, k * TILE : (k + 1) * TILE],
+                    )
+
+        def add(name, index, side, h, value):
+            key = name, h, index, side
+            sums[key] = sums[key] + value if key in sums else value
 
         turn(0)
-        for three in range(heads // 3):
-            some(three)
+        for m in range(ahead):
+            product(m, 0)
+            product(m, 1)
+        for m in range(len(pairs) + 1):
+            three = m // group
+            if m % group == TURN_AT and m + group < len(pairs):
+                turn(three + 1)
+            if m % group == BACK_AT and three > 0:
+                turn_back(three - 1)
+            now = pairs[m] if m < len(pairs) else ()
+            before = pairs[m - 1] if m > 0 else ()
+            product(m + ahead, 0)
+            exps = []
+            for side, (h, j, k) in enumerate(now):
+                first = tile_start(j) + k * TILE
+                e = exponents[l, h, first : first + TILE, :]
+                parts = [
+                    e[p * half : (p + 1) * half] * products.pop((m, side, p)).astype(bfloat)
+                    for p in range(2)
+                ]
+                grad_score = jnp.concatenate(parts, axis=0)
+                flipped[m % 2, side] = grad_score.T
+                held[m, side] = grad_score
+                exps.append(e)
+            for side, (h, j, k) in enumerate(now):
+                js = slice(j * TILE, (j + 1) * TILE)
+                add("v", k, side, h, dot(grad_att[h, :HEAD, js], exps[side]))
+            product(m + ahead, 1)
+            for side, (h, j, k) in enumerate(before):
+                js = slice(j * TILE, (j + 1) * TILE)
+                add("k", k, side, h, dot(queries[l, h, :, js], held.pop((m - 1, side))))
+            for side, (h, j, k) in enumerate(before):
+                ks = slice(k * TILE, (k + 1) * TILE)
+                add("q", j, side, h, dot(keys[l, h, :, ks], flipped[(m - 1) % 2, side]))
+            if m > 0 and m % group == 0:
+                for h in range((three - 1) * 3, three * 3):
+                    for name, ref in (("q", grad_q), ("k", grad_k), ("v", grad_proj)):
+                        for t in range(tiles):
+                            found = [sums.pop((name, h, t, n), None) for n in range(2)]
+                            found = [f for f in found if f is not None]
+                            place = h + 2 * heads if name == "v" else h
+                            total = sum(found[1:], found[0]).astype(ref.dtype)
+                            ref[place, :, t * TILE : (t + 1) * TILE] = total
         turn_back(heads // 3 - 1)
 
-        for cs in chunks:
-            low = grad_proj[:, :, cs].reshape(3 * width, CHUNK)
-            grad_normed = dot(qkv_w[l], low)
+        lows = [grad_proj[:, :, cs].reshape(3 * width, CHUNK) for cs in chunks]
+        grad_normeds = [dot(qkv_w[l], low) for low in lows]
+        grad_qkv[slot] += dot_nt(normed[l], grad_proj[...].reshape(3 * width, length))
+        for cs, grad_normed in zip(chunks, grad_normeds):
             u, inv = inputs[l, :, cs], inverse1[l, :, cs]
             grad_u, partial = rms_backward(grad_normed, u, inv, gain_of(l, 0))
             grad_gains[slot, 0] += partial
             grad_u = grad_u + grad[:, cs]
             grad[:, cs] = grad_u.astype(bfloat).astype(single)
             grad_inputs[l, :, cs] = grad_u
-        grad_qkv[slot] += dot_nt(normed[l], grad_proj[...].reshape(3 * width, length))
         return carry
 
     lax.fori_loop(0, 2, backward, 0)
@@ -489,7 +490,8 @@
     width, length = raw.shape[1:]
     heads = width // HEAD
     hidden = own[4].shape[1]
-    place = jnp.stack([section, section * count]).astype(jnp.int32)
+    here = jnp.reshape(section, (1,)).astype(jnp.int32)
+    start = jnp.reshape(section * count, (1,)).astype(jnp.int32)
     tables = jnp.asarray(rotary_tables(length))
     operands = (raw, cotangent) + own + other + (tables,)
     smem = pl.BlockSpec(memory_space=pltpu.SMEM)
@@ -500,7 +502,7 @@
             array.shape, lambda i, *_: zeros, pipeline_mode=pl.Buffered(buffer_count=1)
         )
 
-    placed_block = pl.BlockSpec((1, width, length), lambda i, place, ids: (place[1] + i, 0, 0))
+    placed_block = pl.BlockSpec((1, width, length), lambda i, here, start, ids: (start[0] + i, 0, 0))
     block = pl.BlockSpec((1, width, length), lambda i, *_: (i, 0, 0))
     shape = jax.ShapeDtypeStruct
     totals = (shape((rows, 128), single), shape((rows, 128), bfloat))
@@ -551,7 +553,7 @@
     return pl.pallas_call(
         functools.partial(train_kernel, heads, hidden),
         grid_spec=pltpu.PrefetchScalarGridSpec(
-            num_scalar_prefetch=2,
+            num_scalar_prefetch=3,
             grid=(count,),
             in_specs=[smem, smem, placed_block, placed_block] + [whole(a) for a in operands[2:]],
             out_specs=[placed_block, placed_block, block, block] + [whole(t) for t in totals],
@@ -565,7 +567,7 @@
         )
         + totals,
         compiler_params=pltpu.CompilerParams(vmem_limit_bytes=VMEM_LIMIT),
-    )(place, series_ids, median, scale, *operands)
+    )(here, start, series_ids, median, scale, *operands)
 
 
 def partner():
@@ -732,7 +734,7 @@
     layer_outputs[...] = far_out[...]
     input_grads[...] = far_grad[...].astype(single)
 
-    @pl.when(pl.program_id(0) == 0)
+    @pl.when((pl.program_id(0) == 0) & (pl.program_id(1) == 0))
     def _():
         width = grad_qkv.shape[0]
         block = 0
@@ -751,8 +753,9 @@
     shape = jax.ShapeDtypeStruct
     count, width, length = far_out.shape
     anywhere = pl.BlockSpec(memory_space=pl.ANY)
-    block = pl.BlockSpec((1, width, length), lambda i, place: (i, 0, 0))
-    placed = pl.BlockSpec((1, width, length), lambda i, place: (place[0] + i, 0, 0))
+    part = width // 3
+    block = pl.BlockSpec((1, part, length), lambda i, n, place: (i, n, 0))
+    placed = pl.BlockSpec((1, part, length), lambda i, n, place: (place[0] + i, n, 0))
     grads = (
         shape((2, width), single),
         shape((width, 3 * width), single),
@@ -763,14 +766,14 @@
 
     def whole(array):
         return pl.BlockSpec(
-            array.shape, lambda i, place: (0, 0), pipeline_mode=pl.Buffered(buffer_count=1)
+            array.shape, lambda i, n, place: (0, 0), pipeline_mode=pl.Buffered(buffer_count=1)
         )
 
     return pl.pallas_call(
         finish_kernel,
         grid_spec=pltpu.PrefetchScalarGridSpec(
             num_scalar_prefetch=1,
-            grid=(count,),
+            grid=(count, 3),
             in_specs=[whole(gathered), block, block, anywhere, anywhere],
             out_specs=[placed, placed] + [whole(g) for g in grads],
         ),

time: 176 us -> 175 us (level)
    pallas_call x1, Pallas kernels: 135 us -> 131 us  [train(): pl.pallas_call(functools.partial(train_kernel, heads, hidden), grid_spec=...]
    pallas_call x1, Pallas kernels: 4.78 us -> 8.71 us  [finish(): pl.pallas_call(finish_kernel, grid_spec=pltpu.PrefetchScalarGridSpec(num_...]
where the time goes in v6:
time: 175 us
  Pallas kernels  174 us (99%)
    pallas_call x1, Pallas kernels, train(): pl.pallas_call(functools.partial(train_kernel, heads, hidden), grid_spec=...  131 us
    pallas_call x1, Pallas kernels, reduce(): pl.pallas_call(functools.partial(reduce_kernel, sizes), out_shape=(shape(...  32 us
    pallas_call x1, Pallas kernels, finish(): pl.pallas_call(finish_kernel, grid_spec=pltpu.PrefetchScalarGridSpec(num_...  8.71 us

profile of v6, /device:TPU:0, one launch (start us, length us, event | category | flops | bytes accessed | tf_op | source)
XLA Modules:
  0.0 174.8 jit_solution(18288025449112662826)
XLA Ops:
  0.6 2.5 %shard_map.162 = (f32[2,144]{1,0:T(2,128)}, bf16[144,432]{1,0:T(8,128)(2,1)}, bf16[144,144]{1,0:T(8,128)(2,1)}, bf16[144,768]{1,0:T(8,128)(2,1)}, bf16[144,384]{1,0:T(8,128)(2,1)}) custom-call(f32[2,144]{1,0:T(2,128)} %bitcast.37, bf16[144,432]{1,0:T(8,128)(2,1)} %bitcast.31, bf16[144,144]{1,0:T(8,128)(2,1)} %bitcast.35, bf16[144,768]{1,0:T(8,128)(2,1)} %bitcast.29, ...), custom_call_target="tpu_custom_call" | custom-call | tf_op jit(solution)/shard_map/pallas_call | solution.py:607
  3.2 130.9 %shard_map.163 = (bf16[8,144,1024]{2,1,0:T(8,128)(2,1)}, f32[8,144,1024]{2,1,0:T(8,128)}, bf16[4,144,1024]{2,1,0:T(8,128)(2,1)}, bf16[4,144,1024]{2,1,0:T(8,128)...) custom-call(s32[1]{0:T(128)} %bitcast.1.here, s32[1]{0:T(128)} %bitcast.2.start, s32[8]{0:T(128)} %series_ids.1, ...), custom_call_target="tpu_custom_call" | custom-call | tf_op jit(solution)/shard_map/pallas_call | solution.py:553
  134.1 32.0 %shard_map.164 = (bf16[4,144,1024]{2,1,0:T(8,128)(2,1)}, bf16[4,144,1024]{2,1,0:T(8,128)(2,1)}, bf16[2048,128]{1,0:T(8,128)(2,1)}) custom-call(f32[2048,128]{1,0:T(8,128)} %get-tuple-element.33.own_total, bf16[2048,128]{1,0:T(8,128)(2,1)} %get-tuple-element.34.other_total, bf16[4,144,1024]{2,1,0:T(8,128)(2,1)} %get-tuple-element.35.sent_out, ...), custom_call_target="tpu_custom_call" | custom-call | tf_op jit(solution)/shard_map/pallas_call | solution.py:800
  166.1 8.7 %shard_map.165 = (bf16[8,144,1024]{2,1,0:T(8,128)(2,1)}, f32[8,144,1024]{2,1,0:T(8,128)}, f32[2,144]{1,0:T(2,128)}, f32[144,432]{1,0:T(8,128)}, f32[144,144]{1,0...) custom-call(s32[1]{0:T(128)} %bitcast.place, ...), custom_call_target="tpu_custom_call", output_to_operand_aliasing={{0}: (4, {}), {1}: (5, {})} | custom-call | tf_op jit(solution)/shard_map/pallas_call | solution.py:772

commit v7 on v6

--- a/solution.py
+++ b/solution.py
@@ -717,8 +717,7 @@
 
 
 def finish_kernel(
-    place,
-    gathered,
+    gathered_far,
     far_out,
     far_grad,
     kept_out,
@@ -730,57 +729,76 @@
     grad_out,
     grad_gate_up,
     grad_down,
+    gathered,
+    passed,
+    narrow,
+    wide,
+    arrive,
+    leave,
 ):
-    layer_outputs[...] = far_out[...]
-    input_grads[...] = far_grad[...].astype(single)
-
-    @pl.when((pl.program_id(0) == 0) & (pl.program_id(1) == 0))
-    def _():
-        width = grad_qkv.shape[0]
-        block = 0
-        for ref in (grad_gate_up, grad_down, grad_qkv, grad_out):
-            for n in range(0, ref.shape[1] - 127, 128):
-                rows = slice(block * width, (block + 1) * width)
-                ref[:, n : n + 128] = gathered[rows, :].astype(single)
-                block += 1
-        rest = gathered[block * width : (block + 1) * width, :].astype(single)
-        grad_qkv[:, 3 * width - QKV_REST :] = rest[:, :QKV_REST]
-        grad_out[:, width - OUT_REST :] = rest[:, QKV_REST : QKV_REST + OUT_REST]
-        grad_gains[...] = rest.T[QKV_REST + OUT_REST : QKV_REST + OUT_REST + 2, :]
-
-
-def finish(place, gathered, far_out, far_grad, kept_out, kept_grad, hidden):
+    count = far_out.shape[0]
+    place = (1 - lax.axis_index("section")) * count
+    outs = pltpu.make_async_copy(passed, layer_outputs.at[pl.ds(place, count)], leave.at[count])
+    into = pltpu.make_async_copy(far_out, passed, arrive.at[count + 1])
+    sums = pltpu.make_async_copy(gathered_far, gathered, arrive.at[count])
+    reads = [pltpu.make_async_copy(far_grad.at[i], narrow.at[i], arrive.at[i]) for i in range(count)]
+    writes = [
+        pltpu.make_async_copy(wide.at[i], input_grads.at[place + i], leave.at[i])
+        for i in range(count)
+    ]
+    for c in reads + [sums, into]:
+        c.start()
+    for i in range(count):
+        reads[i].wait()
+        wide[i] = narrow[i].astype(single)
+        writes[i].start()
+    into.wait()
+    outs.start()
+    sums.wait()
+    width = grad_qkv.shape[0]
+    block = 0
+    for ref in (grad_gate_up, grad_down, grad_qkv, grad_out):
+        for n in range(0, ref.shape[1] - 127, 128):
+            ref[:, n : n + 128] = gathered[block * width : (block + 1) * width, :].astype(single)
+            block += 1
+    rest = gathered[block * width : (block + 1) * width, :].astype(single)
+    grad_qkv[:, 3 * width - QKV_REST :] = rest[:, :QKV_REST]
+    grad_out[:, width - OUT_REST :] = rest[:, QKV_REST : QKV_REST + OUT_REST]
+    grad_gains[...] = rest.T[QKV_REST + OUT_REST : QKV_REST + OUT_REST + 2, :]
+    for c in writes + [outs]:
+        c.wait()
+
+
+def finish(gathered, far_out, far_grad, kept_out, kept_grad, hidden):
     shape = jax.ShapeDtypeStruct
     count, width, length = far_out.shape
     anywhere = pl.BlockSpec(memory_space=pl.ANY)
-    part = width // 3
-    block = pl.BlockSpec((1, part, length), lambda i, n, place: (i, n, 0))
-    placed = pl.BlockSpec((1, part, length), lambda i, n, place: (place[0] + i, n, 0))
-    grads = (
-        shape((2, width), single),
-        shape((width, 3 * width), single),
-        shape((width, width), single),
-        shape((width, 2 * hidden), single),
-        shape((width, hidden), single),
-    )
-
-    def whole(array):
-        return pl.BlockSpec(
-            array.shape, lambda i, n, place: (0, 0), pipeline_mode=pl.Buffered(buffer_count=1)
-        )
-
+    vmem = pl.BlockSpec(memory_space=pltpu.VMEM)
+    v = pltpu.VMEM
     return pl.pallas_call(
         finish_kernel,
-        grid_spec=pltpu.PrefetchScalarGridSpec(
-            num_scalar_prefetch=1,
-            grid=(count, 3),
-            in_specs=[whole(gathered), block, block, anywhere, anywhere],
-            out_specs=[placed, placed] + [whole(g) for g in grads],
+        out_shape=(
+            shape(kept_out.shape, bfloat),
+            shape(kept_grad.shape, single),
+            shape((2, width), single),
+            shape((width, 3 * width), single),
+            shape((width, width), single),
+            shape((width, 2 * hidden), single),
+            shape((width, hidden), single),
         ),
-        out_shape=(shape(kept_out.shape, bfloat), shape(kept_grad.shape, single)) + grads,
-        input_output_aliases={4: 0, 5: 1},
+        in_specs=[anywhere] * 5,
+        out_specs=[anywhere] * 2 + [vmem] * 5,
+        scratch_shapes=[
+            v(gathered.shape, bfloat),
+            v(far_out.shape, bfloat),
+            v(far_grad.shape, bfloat),
+            v(far_grad.shape, single),
+            pltpu.SemaphoreType.DMA((count + 2,)),
+            pltpu.SemaphoreType.DMA((count + 1,)),
+        ],
+        input_output_aliases={3: 0, 4: 1},
         compiler_params=pltpu.CompilerParams(vmem_limit_bytes=VMEM_LIMIT),
-    )(place, gathered, far_out, far_grad, kept_out, kept_grad)
+    )(gathered, far_out, far_grad, kept_out, kept_grad)
 
 
 def reduce(devices, own_total, other_total, sent_out, sent_grad):
@@ -843,9 +861,8 @@
         section, rows, turned(raw), series_ids, median, scale, turned(cotangent), own, other
     )
     far_out, far_grad, gathered = reduce(devices, own_total, other_total, sent_out, sent_grad)
-    place = jnp.reshape((1 - section) * count, (1,)).astype(jnp.int32)
     layer_outputs, input_grads, gain, qkv, out, gate_up, down = finish(
-        place, gathered, far_out, far_grad, kept_out, kept_grad, hidden
+        gathered, far_out, far_grad, kept_out, kept_grad, hidden
     )
     return (
         turned(layer_outputs)[None],

time: 175 us -> 170 us (0.971)
  Pallas kernels: 174 us -> 169 us
    pallas_call x1, Pallas kernels: 8.71 us -> 3.89 us  [finish(): pl.pallas_call(finish_kernel, out_shape=(shape(kept_out.shape, bfloat), s...]
where the time goes in v7:
time: 170 us
  Pallas kernels  169 us (99%)
    pallas_call x1, Pallas kernels, train(): pl.pallas_call(functools.partial(train_kernel, heads, hidden), grid_spec=...  131 us
    pallas_call x1, Pallas kernels, reduce(): pl.pallas_call(functools.partial(reduce_kernel, sizes), out_shape=(shape(...  32 us
    pallas_call x1, Pallas kernels, finish(): pl.pallas_call(finish_kernel, out_shape=(shape(kept_out.shape, bfloat), s...  3.89 us

profile of v7, /device:TPU:0, one launch (start us, length us, event | category | flops | bytes accessed | tf_op | source)
XLA Modules:
  0.0 169.9 jit_solution(13671374800604184577)
XLA Ops:
  0.6 2.5 %shard_map.162 = (f32[2,144]{1,0:T(2,128)}, bf16[144,432]{1,0:T(8,128)(2,1)}, bf16[144,144]{1,0:T(8,128)(2,1)}, bf16[144,768]{1,0:T(8,128)(2,1)}, bf16[144,384]{1,0:T(8,128)(2,1)}) custom-call(f32[2,144]{1,0:T(2,128)} %bitcast.36, bf16[144,432]{1,0:T(8,128)(2,1)} %bitcast.30, bf16[144,144]{1,0:T(8,128)(2,1)} %bitcast.34, bf16[144,768]{1,0:T(8,128)(2,1)} %bitcast.28, ...), custom_call_target="tpu_custom_call" | custom-call | tf_op jit(solution)/shard_map/pallas_call | solution.py:607
  3.1 130.9 %shard_map.163 = (bf16[8,144,1024]{2,1,0:T(8,128)(2,1)}, f32[8,144,1024]{2,1,0:T(8,128)}, bf16[4,144,1024]{2,1,0:T(8,128)(2,1)}, bf16[4,144,1024]{2,1,0:T(8,128)...) custom-call(s32[1]{0:T(128)} %bitcast.here, s32[1]{0:T(128)} %bitcast.1.start, s32[8]{0:T(128)} %series_ids.1, ...), custom_call_target="tpu_custom_call" | custom-call | tf_op jit(solution)/shard_map/pallas_call | solution.py:553
  134.1 32.0 %shard_map.164 = (bf16[4,144,1024]{2,1,0:T(8,128)(2,1)}, bf16[4,144,1024]{2,1,0:T(8,128)(2,1)}, bf16[2048,128]{1,0:T(8,128)(2,1)}) custom-call(f32[2048,128]{1,0:T(8,128)} %get-tuple-element.33.own_total, bf16[2048,128]{1,0:T(8,128)(2,1)} %get-tuple-element.34.other_total, bf16[4,144,1024]{2,1,0:T(8,128)(2,1)} %get-tuple-element.35.sent_out, ...), custom_call_target="tpu_custom_call" | custom-call | tf_op jit(solution)/shard_map/pallas_call | solution.py:818
  166.1 3.9 %shard_map.165 = (bf16[8,144,1024]{2,1,0:T(8,128)(2,1)}, f32[8,144,1024]{2,1,0:T(8,128)}, f32[2,144]{1,0:T(2,128)}, f32[144,432]{1,0:T(8,128)}, f32[144,144]{1,0...) custom-call(bf16[2048,128]{1,0:T(8,128)(2,1)} %get-tuple-element.37.gathered_far,, ...), custom_call_target="tpu_custom_call", output_to_operand_aliasing={{0}: (3, {}), {1}: (4, {})} | custom-call | tf_op jit(solution)/shard_map/pallas_call | solution.py:778

commit v8 on v7

--- a/solution.py
+++ b/solution.py
@@ -13,7 +13,7 @@
 HALF = HEAD // 2
 TILE = 256
 CHUNK = 512
-ROWS = 128
+ROWS = 384
 TURN_AT = 6
 BACK_AT = 8
 VMEM_LIMIT = 64 * 2**20 - 2**16
@@ -404,7 +404,7 @@
                 first = tile_start(j) + k * TILE
                 e = exponents[l, h, first : first + TILE, :]
                 parts = [
-                    e[p * half : (p + 1) * half] * products.pop((m, side, p)).astype(bfloat)
+                    (e[p * half : (p + 1) * half].astype(single) * products.pop((m, side, p))).astype(bfloat)
                     for p in range(2)
                 ]
                 grad_score = jnp.concatenate(parts, axis=0)
@@ -635,6 +635,8 @@
     far_grad,
     gathered,
     arrived,
+    kept_total,
+    local,
     *scratch,
 ):
     count = len(sizes)
@@ -654,6 +656,8 @@
         places.append(place)
         groups.append(peers)
         stride *= size
+    loaded = pltpu.make_async_copy(own_total, kept_total, local)
+    loaded.start()
     meet([partner()] + [device for peers in groups for _, device in peers])
 
     def copy(source, target, send, recv, device):
@@ -674,7 +678,8 @@
         copy(sent_out, far_out, swap_send.at[1], swap_recv.at[1], partner()),
         copy(sent_grad, far_grad, swap_send.at[2], swap_recv.at[2], partner()),
     ]
-    parts[0][...] = (own_total[...] + arrived[...].astype(single)).astype(bfloat)
+    loaded.wait()
+    parts[0][...] = (kept_total[...] + arrived[...].astype(single)).astype(bfloat)
     first = 0
     starts = []
     for n, size in enumerate(sizes):
@@ -822,9 +827,9 @@
             shape(sent_grad.shape, bfloat),
             shape((rows, 128), bfloat),
         ),
-        in_specs=[vmem, vmem, anywhere, anywhere],
+        in_specs=[anywhere] * 4,
         out_specs=[anywhere, anywhere, vmem],
-        scratch_shapes=[v((rows, 128), bfloat)]
+        scratch_shapes=[v((rows, 128), bfloat), v((rows, 128), single), dma]
         + parts
         + slots
         + parts[1:]

time: 170 us -> 168 us (0.988)
  Pallas kernels: 169 us -> 167 us
where the time goes in v8:
time: 168 us
  Pallas kernels  167 us (99%)
    pallas_call x1, Pallas kernels, train(): pl.pallas_call(functools.partial(train_kernel, heads, hidden), grid_spec=...  130 us
    pallas_call x1, Pallas kernels, reduce(): pl.pallas_call(functools.partial(reduce_kernel, sizes), out_shape=(shape(...  31 us
    pallas_call x1, Pallas kernels, finish(): pl.pallas_call(finish_kernel, out_shape=(shape(kept_out.shape, bfloat), s...  3.89 us

profile of v8, /device:TPU:0, one launch (start us, length us, event | category | flops | bytes accessed | tf_op | source)
XLA Modules:
  0.0 167.9 jit_solution(6371571362323580075)
XLA Ops:
  0.6 2.5 %shard_map.162 = (f32[2,144]{1,0:T(2,128)}, bf16[144,432]{1,0:T(8,128)(2,1)}, bf16[144,144]{1,0:T(8,128)(2,1)}, bf16[144,768]{1,0:T(8,128)(2,1)}, bf16[144,384]{1,0:T(8,128)(2,1)}) custom-call(f32[2,144]{1,0:T(2,128)} %bitcast.36, bf16[144,432]{1,0:T(8,128)(2,1)} %bitcast.30, bf16[144,144]{1,0:T(8,128)(2,1)} %bitcast.34, bf16[144,768]{1,0:T(8,128)(2,1)} %bitcast.28, ...), custom_call_target="tpu_custom_call" | custom-call | tf_op jit(solution)/shard_map/pallas_call | solution.py:607
  3.1 129.8 %shard_map.163 = (bf16[8,144,1024]{2,1,0:T(8,128)(2,1)}, f32[8,144,1024]{2,1,0:T(8,128)}, bf16[4,144,1024]{2,1,0:T(8,128)(2,1)}, bf16[4,144,1024]{2,1,0:T(8,128)...) custom-call(s32[1]{0:T(128)} %bitcast.here, s32[1]{0:T(128)} %bitcast.1.start, s32[8]{0:T(128)} %series_ids.1, ...), custom_call_target="tpu_custom_call" | custom-call | tf_op jit(solution)/shard_map/pallas_call | solution.py:553
  133.0 31.0 %shard_map.164 = (bf16[4,144,1024]{2,1,0:T(8,128)(2,1)}, bf16[4,144,1024]{2,1,0:T(8,128)(2,1)}, bf16[2048,128]{1,0:T(8,128)(2,1)}) custom-call(f32[2048,128]{1,0:T(8,128)} %get-tuple-element.33.own_total, bf16[2048,128]{1,0:T(8,128)(2,1)} %get-tuple-element.34.other_total, bf16[4,144,1024]{2,1,0:T(8,128)(2,1)} %get-tuple-element.35.sent_out, ...), custom_call_target="tpu_custom_call" | custom-call | tf_op jit(solution)/shard_map/pallas_call | solution.py:823
  164.0 3.9 %shard_map.165 = (bf16[8,144,1024]{2,1,0:T(8,128)(2,1)}, f32[8,144,1024]{2,1,0:T(8,128)}, f32[2,144]{1,0:T(2,128)}, f32[144,432]{1,0:T(8,128)}, f32[144,144]{1,0...) custom-call(bf16[2048,128]{1,0:T(8,128)(2,1)} %get-tuple-element.37.gathered_far,, ...), custom_call_target="tpu_custom_call", output_to_operand_aliasing={{0}: (3, {}), {1}: (4, {})} | custom-call | tf_op jit(solution)/shard_map/pallas_call | solution.py:783

commit v9 on v8

--- a/solution.py
+++ b/solution.py
@@ -14,7 +14,7 @@
 TILE = 256
 CHUNK = 512
 ROWS = 384
-TURN_AT = 6
+TURN_AT = 9
 BACK_AT = 8
 VMEM_LIMIT = 64 * 2**20 - 2**16
 EPSILON = 1e-06
@@ -352,7 +352,7 @@
             extra = jnp.where(row == 0, coarse, jnp.where(row == 1, mean - coarse, 0.0))
             rest = jnp.zeros((heads, HALF, CHUNK), single)
             grad_att[:, :, cs] = jnp.concatenate([back * inverse, extra, rest], axis=1).astype(bfloat)
-        grad_down[slot] += dot_nt(grad_low[...], activated[l])
+        grad_down[slot] += dot_nt(activated[l], grad_low[...])
         grad_out[slot] += dot_nt(attended[l].reshape(width, length), grad_res_low[...])
 
         def turn(three):
@@ -416,11 +416,11 @@
                 add("v", k, side, h, dot(grad_att[h, :HEAD, js], exps[side]))
             product(m + ahead, 1)
             for side, (h, j, k) in enumerate(before):
+                ks = slice(k * TILE, (k + 1) * TILE)
+                add("q", j, side, h, dot(keys[l, h, :, ks], flipped[(m - 1) % 2, side]))
+            for side, (h, j, k) in enumerate(before):
                 js = slice(j * TILE, (j + 1) * TILE)
                 add("k", k, side, h, dot(queries[l, h, :, js], held.pop((m - 1, side))))
-            for side, (h, j, k) in enumerate(before):
-                ks = slice(k * TILE, (k + 1) * TILE)
-                add("q", j, side, h, dot(keys[l, h, :, ks], flipped[(m - 1) % 2, side]))
             if m > 0 and m % group == 0:
                 for h in range((three - 1) * 3, three * 3):
                     for name, ref in (("q", grad_q), ("k", grad_k), ("v", grad_proj)):
@@ -457,9 +457,10 @@
         for slot, total in ((0, own_total), (1, other_total)):
             blocks = []
             for ref in (grad_gate_up, grad_down, grad_qkv, grad_out):
-                for n in range(0, ref.shape[2] - 127, 128):
+                sums = ref[slot].T if ref is grad_down else ref[slot]
+                for n in range(0, sums.shape[1] - 127, 128):
                     doubled = ref is grad_gate_up and n < hidden
-                    blocks.append(ref[slot, :, n : n + 128] * (0.5 if doubled else 1.0))
+                    blocks.append(sums[:, n : n + 128] * (0.5 if doubled else 1.0))
             lane = lax.broadcasted_iota(jnp.int32, (width, 128), 1)
             spare = grad_qkv[slot, :, 3 * width - QKV_REST :]
             out_rest = grad_out[slot, :, width - OUT_REST :]
@@ -522,7 +523,7 @@
         v((2, width, 3 * width), single),
         v((2, width, width), single),
         v((2, width, 2 * hidden), single),
-        v((2, width, hidden), single),
+        v((2, hidden, width), single),
         v((3, width, length), single),
         v((2, 1, length), single),
         v((2, width, length), bfloat),
@@ -673,7 +674,8 @@
         return c
 
     near = copy(other_total, arrived, swap_send.at[0], swap_recv.at[0], partner())
-    near.wait()
+    near.wait_recv()
+    sent = [near]
     far = [
         copy(sent_out, far_out, swap_send.at[1], swap_recv.at[1], partner()),
         copy(sent_grad, far_grad, swap_send.at[2], swap_recv.at[2], partner()),
@@ -697,8 +699,9 @@
             )
         total = parts[n][pl.ds(pl.multiple_of(places[n] * chunk, 16), chunk), :].astype(single)
         for turn, c in enumerate(copies):
-            c.wait()
+            c.wait_recv()
             total = total + slots[n][turn].astype(single)
+        sent += copies
         target = parts[n + 1] if n + 1 < count else last
         target[...] = total.astype(bfloat)
         starts.append(first)
@@ -715,8 +718,11 @@
             )
         wholes[n][mine, :] = source[...]
         for c in copies:
-            c.wait()
+            c.wait_recv()
+        sent += copies
         source = wholes[n]
+    for c in sent:
+        c.wait_send()
     for c in far:
         c.wait()
 

time: 168 us -> 167 us (level)
  no operation moved by 1% of the time
where the time goes in v9:
time: 167 us
  Pallas kernels  166 us (99%)
    pallas_call x1, Pallas kernels, train(): pl.pallas_call(functools.partial(train_kernel, heads, hidden), grid_spec=...  128 us
    pallas_call x1, Pallas kernels, reduce(): pl.pallas_call(functools.partial(reduce_kernel, sizes), out_shape=(shape(...  31.5 us
    pallas_call x1, Pallas kernels, finish(): pl.pallas_call(finish_kernel, out_shape=(shape(kept_out.shape, bfloat), s...  3.89 us

profile of v9, /device:TPU:0, one launch (start us, length us, event | category | flops | bytes accessed | tf_op | source)
XLA Modules:
  0.0 167.0 jit_solution(5213897611065561676)
XLA Ops:
  0.6 2.5 %shard_map.162 = (f32[2,144]{1,0:T(2,128)}, bf16[144,432]{1,0:T(8,128)(2,1)}, bf16[144,144]{1,0:T(8,128)(2,1)}, bf16[144,768]{1,0:T(8,128)(2,1)}, bf16[144,384]{1,0:T(8,128)(2,1)}) custom-call(f32[2,144]{1,0:T(2,128)} %bitcast.36, bf16[144,432]{1,0:T(8,128)(2,1)} %bitcast.30, bf16[144,144]{1,0:T(8,128)(2,1)} %bitcast.34, bf16[144,768]{1,0:T(8,128)(2,1)} %bitcast.28, ...), custom_call_target="tpu_custom_call" | custom-call | tf_op jit(solution)/shard_map/pallas_call | solution.py:608
  3.1 128.5 %shard_map.163 = (bf16[8,144,1024]{2,1,0:T(8,128)(2,1)}, f32[8,144,1024]{2,1,0:T(8,128)}, bf16[4,144,1024]{2,1,0:T(8,128)(2,1)}, bf16[4,144,1024]{2,1,0:T(8,128)...) custom-call(s32[1]{0:T(128)} %bitcast.here, s32[1]{0:T(128)} %bitcast.1.start, s32[8]{0:T(128)} %series_ids.1, ...), custom_call_target="tpu_custom_call" | custom-call | tf_op jit(solution)/shard_map/pallas_call | solution.py:554
  131.6 31.5 %shard_map.164 = (bf16[4,144,1024]{2,1,0:T(8,128)(2,1)}, bf16[4,144,1024]{2,1,0:T(8,128)(2,1)}, bf16[2048,128]{1,0:T(8,128)(2,1)}) custom-call(f32[2048,128]{1,0:T(8,128)} %get-tuple-element.33.own_total, bf16[2048,128]{1,0:T(8,128)(2,1)} %get-tuple-element.34.other_total, bf16[4,144,1024]{2,1,0:T(8,128)(2,1)} %get-tuple-element.35.sent_out, ...), custom_call_target="tpu_custom_call" | custom-call | tf_op jit(solution)/shard_map/pallas_call | solution.py:829
  163.1 3.9 %shard_map.165 = (bf16[8,144,1024]{2,1,0:T(8,128)(2,1)}, f32[8,144,1024]{2,1,0:T(8,128)}, f32[2,144]{1,0:T(2,128)}, f32[144,432]{1,0:T(8,128)}, f32[144,144]{1,0...) custom-call(bf16[2048,128]{1,0:T(8,128)(2,1)} %get-tuple-element.37.gathered_far,, ...), custom_call_target="tpu_custom_call", output_to_operand_aliasing={{0}: (3, {}), {1}: (4, {})} | custom-call | tf_op jit(solution)/shard_map/pallas_call | solution.py:789
